TPU v7x, 32 devices: a whole 2x2x4 slice. The times are simulated.
32 devices in a mesh: frame: 16 (over z, y, x), mp: 2 (over core).
Axes of the slice: x: 2, y: 2, z: 4, core: 2. Of those that a mesh axis runs over, the one named last changes fastest.
Arguments:
- stream: bfloat16 [16, 1024, 1280], P('frame'), may hold values from -6 to 6
- spatial_qkv: bfloat16 [16, 1024, 3, 1280], P('frame', None, None, 'mp'), may hold values from -30 to 30
- spatial_out_w: bfloat16 [1280, 1280], P('mp'), may hold values from -0.625 to 0.625
- temporal_gain: bfloat16 [1280], replicated, may hold values from 0.5 to 1.5
- temporal_qkv_w: bfloat16 [3, 1280, 1280], P(None, None, 'mp'), may hold values from -0.15625 to 0.15625
- temporal_out_w: bfloat16 [1280, 1280], P('mp'), may hold values from -0.625 to 0.625
- decoder_gain: bfloat16 [1280], replicated, may hold values from 0.5 to 1.5
- decoder_kv_w: bfloat16 [2, 1280, 512], P(None, None, 'mp'), may hold values from -0.15625 to 0.15625
- vertex_queries: bfloat16 [778, 512], P(None, 'mp'), may hold values from -6 to 6
- crop_counts: int32 [16], replicated, may hold values from 0 to 3, as said below
- crop_tiles: int32 [16, 3], replicated, may hold values from 0 to 7
- crop_owner: int32 [16, 3], replicated, may hold values from 0 to 15, as said below
Outputs:
- vertex_features: bfloat16 [64, 512, 778], P('frame', 'mp')
- final_stream: bfloat16 [16, 1024, 1280], P('frame', None, 'mp')
Inputs may be any that keep to these rules, and one draw needn't show every extreme that they name: `crop_counts`: some frame has exactly 3 crops. `crop_owner`: the slots of one frame name different owners; no owner is named by more than 4 live slots, and some owner by exactly 4.
All inputs are finite; a program needn't handle non-finite values.
Results may differ from a plain program's by a relative error of at most 0.028.
Values may be sent and summed in bfloat16 or wider, within the bound.
A program may use at most 128 MiB of HBM per device.

v0:
```python
import jax
import jax.numpy as jnp
from jax import lax
from jax.sharding import PartitionSpec as P

HD = 80
TILE = 128
MAXC = 3
RCAP = 4
DEC_HD = 64
V = 778


def layer_norm(values, gain_row):
    row_mean = jnp.mean(values, axis=-1, keepdims=True)
    centred = values - row_mean
    spread = jnp.mean(centred * centred, axis=-1, keepdims=True)
    return (centred * lax.rsqrt(spread + 1e-06) * gain_row.astype(jnp.float32)).astype(jnp.bfloat16)


def soft_weights(scores):
    row_top = jnp.max(scores, axis=-1, keepdims=True)
    raised = jnp.exp(scores - row_top)
    return (raised / jnp.sum(raised, axis=-1, keepdims=True)).astype(jnp.bfloat16)


def crop_slots(crop_counts, crop_owner):
    frames_all, most = crop_owner.shape
    live_slots = (jnp.arange(most, dtype=jnp.int32)[None, :] < crop_counts[:, None]).reshape(-1)
    owner_flat = crop_owner.reshape(-1)
    owner_hits = (
        (owner_flat[:, None] == jnp.arange(frames_all, dtype=jnp.int32)[None, :])
        & live_slots[:, None]
    ).astype(jnp.int32)
    before = jnp.cumsum(owner_hits, axis=0) - owner_hits
    slot_rank = jnp.sum(before * owner_hits, axis=1)
    return (live_slots, owner_flat * RCAP + slot_rank)


def on_device(
    stream,
    spatial_qkv,
    spatial_out_w,
    temporal_gain,
    temporal_qkv_w,
    temporal_out_w,
    decoder_gain,
    decoder_kv_w,
    vertex_queries,
    crop_counts,
    crop_tiles,
    crop_owner,
):
    patches = stream.shape[1]
    model_width = stream.shape[2]
    local_cols = spatial_qkv.shape[3]
    heads_here = local_cols // HD
    score_scale = HD ** (-0.5)
    spatial_query = spatial_qkv[0, :, 0].reshape(patches, heads_here, HD)
    spatial_key = spatial_qkv[0, :, 1].reshape(patches, heads_here, HD)
    spatial_value = spatial_qkv[0, :, 2].reshape(patches, heads_here, HD)
    scores = (
        jnp.einsum("qhd,khd->hqk", spatial_query, spatial_key, preferred_element_type=jnp.float32)
        * score_scale
    )
    weights = soft_weights(scores)
    spatial_heads = (
        jnp.einsum("hqk,khd->qhd", weights, spatial_value, preferred_element_type=jnp.float32)
        .astype(jnp.bfloat16)
        .reshape(patches, local_cols)
    )
    spatial_part = jnp.dot(spatial_heads, spatial_out_w, preferred_element_type=jnp.float32)
    spatial_total = lax.psum(spatial_part.astype(jnp.bfloat16), "mp").astype(jnp.float32)
    middle = (stream[0].astype(jnp.float32) + spatial_total).astype(jnp.bfloat16)
    normed = layer_norm(middle.astype(jnp.float32), temporal_gain)
    projected = jnp.stack(
        [
            jnp.dot(normed, temporal_qkv_w[which], preferred_element_type=jnp.float32).astype(
                jnp.bfloat16
            )
            for which in range(3)
        ],
        axis=1,
    )[None]
    gathered = lax.all_to_all(projected, "frame", split_axis=1, concat_axis=0, tiled=True)
    frames_all = gathered.shape[0]
    patch_rows = gathered.shape[1]
    temporal_query = gathered[:, :, 0].reshape(frames_all, patch_rows, heads_here, HD)
    temporal_key = gathered[:, :, 1].reshape(frames_all, patch_rows, heads_here, HD)
    temporal_value = gathered[:, :, 2].reshape(frames_all, patch_rows, heads_here, HD)
    frame_scores = (
        jnp.einsum(
            "fphd,gphd->phfg", temporal_query, temporal_key, preferred_element_type=jnp.float32
        )
        * score_scale
    )
    frame_weights = soft_weights(frame_scores)
    mixed_heads = (
        jnp.einsum(
            "phfg,gphd->fphd", frame_weights, temporal_value, preferred_element_type=jnp.float32
        )
        .astype(jnp.bfloat16)
        .reshape(frames_all, patch_rows, local_cols)
    )
    frame_heads = lax.all_to_all(mixed_heads, "frame", split_axis=0, concat_axis=1, tiled=True)
    temporal_part = jnp.dot(frame_heads[0], temporal_out_w, preferred_element_type=jnp.float32)
    temporal_total = lax.psum(temporal_part.astype(jnp.bfloat16), "mp").astype(jnp.float32)
    final_stream = (middle.astype(jnp.float32) + temporal_total).astype(jnp.bfloat16)
    out_cols = model_width // lax.axis_size("mp")
    stream_part = lax.dynamic_slice_in_dim(
        final_stream, lax.axis_index("mp") * out_cols, out_cols, 1
    )[None]
    frame_id = lax.axis_index("frame")
    my_tiles = lax.dynamic_index_in_dim(crop_tiles, frame_id, 0, keepdims=False)
    tile_view = final_stream.reshape(patches // TILE, TILE, model_width)
    crop_rows = jnp.take(tile_view, my_tiles, axis=0)
    crop_norm = layer_norm(crop_rows.astype(jnp.float32), decoder_gain).reshape(
        MAXC * TILE, model_width
    )
    dec_local = decoder_kv_w.shape[2]
    crop_keys = jnp.dot(crop_norm, decoder_kv_w[0], preferred_element_type=jnp.float32).astype(
        jnp.bfloat16
    )
    crop_values = jnp.dot(crop_norm, decoder_kv_w[1], preferred_element_type=jnp.float32).astype(
        jnp.bfloat16
    )
    crop_pairs = jnp.concatenate([crop_keys, crop_values], axis=1).reshape(
        MAXC, TILE, 2 * dec_local
    )
    live_slots, slot_index = crop_slots(crop_counts, crop_owner)
    targets = frame_id * RCAP + jnp.arange(RCAP, dtype=jnp.int32)
    choose = ((slot_index[None, :] == targets[:, None]) & live_slots[None, :]).astype(jnp.float32)
    my_owner = lax.dynamic_index_in_dim(crop_owner, frame_id, 0, keepdims=False)
    my_count = lax.dynamic_index_in_dim(crop_counts, frame_id, 0, keepdims=False)
    my_live = jnp.arange(MAXC, dtype=jnp.int32) < my_count
    to_owner = (
        (my_owner[None, :] == jnp.arange(frames_all, dtype=jnp.int32)[:, None]) & my_live[None, :]
    ).astype(jnp.bfloat16)
    outgoing = jnp.einsum(
        "nm,mtc->ntc", to_owner, crop_pairs, preferred_element_type=jnp.float32
    ).astype(jnp.bfloat16)
    incoming = lax.all_to_all(outgoing, "frame", split_axis=0, concat_axis=0, tiled=True)
    by_frame = choose.reshape(RCAP, frames_all, MAXC).sum(axis=2).astype(jnp.bfloat16)
    slot_pairs = jnp.einsum(
        "rg,gtc->rtc", by_frame, incoming, preferred_element_type=jnp.float32
    ).astype(jnp.bfloat16)
    heads_dec = dec_local // DEC_HD
    slot_keys = slot_pairs[:, :, :dec_local].reshape(RCAP, TILE, heads_dec, DEC_HD)
    slot_values = slot_pairs[:, :, dec_local:].reshape(RCAP, TILE, heads_dec, DEC_HD)
    queries = vertex_queries.reshape(V, heads_dec, DEC_HD)
    vertex_scores = jnp.einsum(
        "vhd,rthd->rhvt", queries, slot_keys, preferred_element_type=jnp.float32
    ) * DEC_HD ** (-0.5)
    vertex_weights = soft_weights(vertex_scores)
    decoded = jnp.einsum(
        "rhvt,rthd->rhdv", vertex_weights, slot_values, preferred_element_type=jnp.float32
    )
    return (decoded.astype(jnp.bfloat16).reshape(RCAP, dec_local, V), stream_part)


def solution(mesh):
    placed = (
        P("frame", None, None),
        P("frame", None, None, "mp"),
        P("mp", None),
        P(),
        P(None, None, "mp"),
        P("mp", None),
        P(),
        P(None, None, "mp"),
        P(None, "mp"),
        P(),
        P(),
        P(),
    )
    return jax.shard_map(
        on_device,
        mesh=mesh,
        in_specs=placed,
        out_specs=(P("frame", "mp", None), P("frame", None, "mp")),
        check_vma=False,
    )
```

profile of v0, /device:TPU:14, one launch (start us, length us, event | category | flops | bytes accessed | tf_op | source)
XLA Modules:
  0.0 422.7 jit_solution(8740589909545566961)
XLA Ops:
  7.2 4.0 fusion.106
  11.3 2.5 copy.99
  13.7 2.4 copy.100
  16.2 1.5 copy.101
  17.6 18.0 %fusion.108 = (f32[8,1024]{1,0:T(8,128)S(1)}, f32[8,1024,1024]{1,2,0:T(8,128)}) fusion(bf16[1024,8,80]{0,2,1:T(8,128)(2,1)} %bitcast.108, bf16[1024,8,80]{0,2,1:T(8,128)(2,1)} %bitcast.109), kind=kOutput, calls=%fused_computation.123 | convolution fusion | flops 1367344128 | bytes 36208640 | tf_op jit(solution)/shard_map/sub | solution.py:23
  35.6 12.4 %fusion.65 = bf16[8,1024,80]{1,2,0:T(8,128)(2,1)S(1)} fusion(bf16[1024,8,80]{0,2,1:T(8,128)(2,1)S(1)} %bitcast.110, f32[8,1024,1024]{1,2,0:T(8,128)} %get-tuple-element.23, f32[8,1024]{1,0:T(8,128)S(1)} %get-tuple-element.22), kind=kOutput, calls=%fused_computation.72 | convolution fusion | flops 1359609856 | bytes 36208640 | tf_op jit(solution)/shard_map/hqk,khd->qhd/dot_general | solution.py:68
  48.0 3.8 convolution_convert_fusion.1
  51.8 0.5 all-reduce.5.cloned.1.call-start
  52.3 0.1 copy-done.6
  52.5 23.0 %all-reduce.3.cloned.1.call-done = bf16[1024,1280]{1,0:T(8,128)(2,1)} async-done(((bf16[1024,1280]{1,0:T(8,128)(2,1)}), bf16[1024,1280]{1,0:T(8,128)(2,1)}) %all-reduce.3.cloned.1.call-update) | async-done | bytes 2621456 | tf_op jit(solution)/shard_map/psum | solution.py:73
  75.5 3.4 convert_reduce_fusion
  79.0 0.8 fusion.13
  79.8 0.9 fusion.15
  80.7 0.5 slice-done.1
  81.1 2.2 fusion.66
  83.4 2.2 fusion.69
  85.6 2.2 fusion.72
  87.8 0.6 maximum_bitcast_fusion
  88.4 3.4 copy.103
  91.7 121.5 %all_to_all.26 = bf16[1,1024,3,640]{3,2,0,1:T(4,128)(2,1)S(1)} all-to-all(bf16[1,1024,3,640]{3,2,0,1:T(4,128)(2,1)S(1)} %copy.103), channel_id=1, replica_groups=mesh['frame'=16,'mp'=2] {'frame'}, dimensions={1} | all-to-all | bytes 7864320 | tf_op jit(solution)/shard_map/all_to_all | solution.py:85
  213.3 23.3 %slice_reduce_fusion.2 = (bf16[16,64,640]{2,1,0:T(8,128)(2,1)}, bf16[16,64,640]{2,1,0:T(8,128)(2,1)}, bf16[16,64,640]{2,1,0:T(8,128)(2,1)}) fusion(bf16[16,64,3,640]{3,2,1,0:T(4,128)(2,1)S(1)} %bitcast.103), kind=kLoop, calls=%fused_computation.39 | loop fusion | bytes 7864320 | tf_op jit(solution)/shard_map/slice | solution.py:90
  236.6 4.6 %reshape_squeeze.22 = bf16[16,64,8,80]{3,2,1,0:T(8,128)(2,1)} reshape(bf16[16,64,640]{2,1,0:T(8,128)(2,1)} %get-tuple-element.13) | data formatting | bytes 2621440 | tf_op jit(solution)/shard_map/reshape;squeeze | solution.py:88
  241.2 4.7 %reshape_squeeze.23 = bf16[16,64,8,80]{3,2,1,0:T(8,128)(2,1)} reshape(bf16[16,64,640]{2,1,0:T(8,128)(2,1)} %get-tuple-element.14) | data formatting | bytes 2621440 | tf_op jit(solution)/shard_map/reshape;squeeze | solution.py:89
  245.9 4.7 %fusion.34 = f32[64,8,16,16]{2,3,1,0:T(8,128)S(1)} fusion(bf16[16,64,8,80]{3,2,1,0:T(8,128)(2,1)} %reshape_squeeze.23, bf16[16,64,8,80]{3,2,1,0:T(8,128)(2,1)} %reshape_squeeze.22), kind=kOutput, calls=%fused_computation.49 | convolution fusion | flops 20971520 | bytes 3145728 | tf_op jit(solution)/shard_map/fphd,gphd->phfg/dot_general | solution.py:92
  250.6 3.5 fusion.109
  254.1 4.8 %reshape_squeeze.21 = bf16[16,64,8,80]{3,2,1,0:T(8,128)(2,1)} reshape(bf16[16,64,640]{2,1,0:T(8,128)(2,1)} %get-tuple-element.12) | data formatting | bytes 2621440 | tf_op jit(solution)/shard_map/reshape;squeeze | solution.py:90
  259.0 4.4 %convert_bitcast_fusion = bf16[16,64,8,80]{3,0,2,1:T(8,128)(2,1)S(1)} fusion(f32[64,8,16,16]{2,3,1,0:T(8,128)} %get-tuple-element.25, f32[64,8,16]{2,1,0:T(8,128)S(1)} %get-tuple-element.24, bf16[16,64,8,80]{3,2,1,0:T(8,128)(2,1)} %reshape_squeeze.21), kind=kOutput, calls=%fused_computation.52 | convolution fusion | flops 21889024 | bytes 3178496 | tf_op jit(solution)/shard_map/phfg,gphd->fphd/dot_general | solution.py:99
  263.4 1.9 copy.111
  265.3 4.2 %reshape.344 = bf16[16,64,640]{2,1,0:T(8,128)(2,1)} reshape(bf16[16,64,8,80]{3,2,1,0:T(8,128)(2,1)} %copy.111) | data formatting | bytes 2621440 | tf_op jit(solution)/shard_map/reshape | solution.py:103
  269.6 35.3 %all_to_all.27 = bf16[16,64,640]{2,1,0:T(8,128)(2,1)S(1)} all-to-all(bf16[16,64,640]{2,1,0:T(8,128)(2,1)} %reshape.344), channel_id=1, replica_groups=mesh['frame'=16,'mp'=2] {'frame'}, dimensions={0} | all-to-all | bytes 2621440 | tf_op jit(solution)/shard_map/all_to_all | solution.py:105
  304.9 3.7 convolution_convert_fusion
  308.7 0.6 copy-done.7
  309.3 0.2 dynamic-slice_reduce_fusion
  309.5 0.6 dynamic_slice.15
  310.1 0.2 dynamic-slice_reduce_fusion.1
  310.3 0.7 iota_compare_fusion.3
  311.0 20.2 %all-reduce.5.cloned.1.call-done = bf16[1024,1280]{1,0:T(8,128)(2,1)} async-done(((bf16[1024,1280]{1,0:T(8,128)(2,1)}), bf16[1024,1280]{1,0:T(8,128)(2,1)}) %all-reduce.5.cloned.1.call-update) | async-done | bytes 2621456 | tf_op jit(solution)/shard_map/psum | solution.py:107
  331.2 3.9 fusion.16
  335.1 2.5 gather_fusion
  337.6 0.3 convert_reduce_fusion.1
  337.9 0.5 fusion.39
  338.4 0.4 fusion.41
  338.8 0.6 convolution_convert_fusion.3
  339.4 0.6 convolution_convert_fusion.4
  340.0 0.2 copy.112
  340.2 0.9 convolution_convert_fusion.2
  341.1 2.5 copy.114
  343.6 7.6 %all-to-all-start.2 = ((bf16[16,128,512]{2,1,0:T(8,128)(2,1)}), bf16[16,128,512]{2,1,0:T(8,128)(2,1)}, u32[]{:S(2)}, u32[]{:S(2)}) async-start(bf16[16,128,512]{2,1,0:T(8,128)(2,1)} %copy.114), calls=%async_computation.2 | async-start | bytes 4194304 | tf_op jit(solution)/shard_map/all_to_all | solution.py:142
  351.2 0.1 copy.96
  351.4 0.1 lt.62
  351.5 0.1 copy.98
  351.6 0.1 eq.44
  351.9 0.2 select_reduce_fusion
  352.1 0.1 copy.97
  352.2 0.3 copy.118
  352.6 1.2 dynamic-slice_bitcast_fusion
  353.8 45.8 %all-to-all-done.2 = bf16[16,128,512]{2,1,0:T(8,128)(2,1)} async-done(((bf16[16,128,512]{2,1,0:T(8,128)(2,1)}), bf16[16,128,512]{2,1,0:T(8,128)(2,1)}, u32[]{:S(2)}, u32[]{:S(2)}) %all-to-all-start.2) | async-done | bytes 2097184 | tf_op jit(solution)/shard_map/all_to_all | solution.py:142
  399.6 2.9 fusion.75
  402.5 0.2 fusion.107
  402.7 0.2 copy.117
  402.9 0.9 copy.116
  403.8 4.8 %fusion.110 = (f32[4,4,778]{2,0,1:T(4,128)S(1)}, f32[4,4,778,128]{3,2,0,1:T(8,128)}) fusion(bf16[778,4,64,1]{0,2,3,1:T(8,128)(2,1)S(1)} %bitcast.107, bf16[4,128,4,64]{1,3,2,0:T(8,128)(2,1)S(1)} %bitcast.112), kind=kOutput, calls=%fused_computation.125 | convolution fusion | flops 208728192 | bytes 7083648 | tf_op jit(solution)/shard_map/sub | solution.py:23
  408.6 4.4 %fusion.44 = bf16[4,4,64,778]{3,2,1,0:T(8,128)(2,1)S(1)} fusion(bf16[4,128,4,64]{1,3,2,0:T(8,128)(2,1)} %bitcast.115, f32[4,4,778,128]{3,2,0,1:T(8,128)} %get-tuple-element.27, f32[4,4,778]{2,0,1:T(4,128)S(1)} %get-tuple-element.26), kind=kOutput, calls=%fused_computation.59 | convolution fusion | flops 207931392 | bytes 8278656 | tf_op jit(solution)/shard_map/rhvt,rthd->rhdv/dot_general | solution.py:155
  413.0 2.4 copy.121
  (46 shorter events, 0.6 us)
Async XLA Ops:
  7.2 40.8 %copy-start = (bf16[640,1280]{1,0:T(8,128)(2,1)S(1)}, bf16[640,1280]{1,0:T(8,128)(2,1)}, u32[]{:S(2)}) copy-start(bf16[640,1280]{1,0:T(8,128)(2,1)} %param.14) | copy-start | bytes 4915204
  7.2 68.3 %all-reduce.3.cloned.1.call-start = ((), (), s32[]{:S(2)}) async-start(), calls=%async_computation.3 | async-start | bytes 5242880 | tf_op jit(solution)/shard_map/psum | solution.py:73
  17.6 18.0 %copy-start.3 = (bf16[1,1024,1,640]{1,3,2,0:T(8,128)(2,1)S(1)}, bf16[1,1024,1,640]{1,3,2,0:T(8,128)(2,1)}, u32[]{:S(2)}) copy-start(bf16[1,1024,1,640]{1,3,2,0:T(8,128)(2,1)} %copy.101) | copy-start | bytes 3932164
  51.8 0.7 copy-start.6
  51.8 279.4 %all-reduce.5.cloned.1.call-start = ((), (), s32[]{:S(2)}) async-start(), calls=%async_computation.4 | async-start | bytes 5242880 | tf_op jit(solution)/shard_map/psum | solution.py:107
  75.5 5.2 %slice-start = ((s8[4915200]{0:T(1024)(128)(4,1)}), s8[720896]{0:T(1024)(128)(4,1)S(1)}, s32[]{:S(2)}) async-start(s8[4915200]{0:T(1024)(128)(4,1)} %bitcast.116), calls=%async_computation.5 | async-start | bytes 1441792
  78.9 2.2 slice-start.1
  269.6 35.3 %copy-start.10 = (bf16[640,1280]{1,0:T(8,128)(2,1)S(1)}, bf16[640,1280]{1,0:T(8,128)(2,1)}, u32[]{:S(2)}) copy-start(bf16[640,1280]{1,0:T(8,128)(2,1)} %param.17) | copy-start | bytes 4915204
  308.6 0.7 copy-start.7
  308.6 0.7 copy-start.8
  308.6 0.9 copy-start.9
  308.6 1.5 copy-start.5
  335.1 3.7 copy-start.11
  343.6 8.6 %copy-start.4 = (bf16[778,256]{1,0:T(8,128)(2,1)S(1)}, bf16[778,256]{1,0:T(8,128)(2,1)}, u32[]{:S(2)}) copy-start(bf16[778,256]{1,0:T(8,128)(2,1)} %param.20) | copy-start | bytes 1195012
  343.6 9.0 %copy-start.2 = (bf16[1024,1280]{1,0:T(8,128)(2,1)S(1)}, bf16[1024,1280]{1,0:T(8,128)(2,1)}, u32[]{:S(2)}) copy-start(bf16[1024,1280]{1,0:T(8,128)(2,1)} %fusion.16) | copy-start | bytes 7864324
  343.6 56.0 %all-to-all-start.2 = ((bf16[16,128,512]{2,1,0:T(8,128)(2,1)}), bf16[16,128,512]{2,1,0:T(8,128)(2,1)}, u32[]{:S(2)}, u32[]{:S(2)}) async-start(bf16[16,128,512]{2,1,0:T(8,128)(2,1)} %copy.114), calls=%async_computation.2 | async-start | bytes 4194304 | tf_op jit(solution)/shard_map/all_to_all | solution.py:142
  408.6 6.8 %copy-start.1 = (bf16[640,1280]{1,0:T(8,128)(2,1)S(1)}, bf16[640,1280]{1,0:T(8,128)(2,1)}, u32[]{:S(2)}) copy-start(bf16[640,1280]{1,0:T(8,128)(2,1)} %param.14) | copy-start | bytes 4915204
Sparse Core Ops, SparseCore 0:
  51.9 23.5 all-reduce.2
  308.8 22.3 all-reduce.4
where the time goes:
time: 431 us; the launch traced here: 423 us
  blocking collectives  157 us (36%)
  waiting for transfers between devices  89.1 us (21%)
  local copies, waits for them, and re-layouts  70.5 us (16%)
  matrix products  67.7 us (16%)
  other arithmetic  15.5 us (4%)
  between operations  14.8 us (3%)
  starting transfers between devices  8.17 us (2%)
    all_to_all x1, blocking collectives, on_device(): lax.all_to_all(projected, 'frame', split_axis=1, concat_axis=0, tiled=True)  122 us
    all_to_all x1, waiting for transfers between devices, on_device(): lax.all_to_all(outgoing, 'frame', split_axis=0, concat_axis=0, tiled=True)  45.8 us
    all_to_all x1, blocking collectives, on_device(): lax.all_to_all(mixed_heads, 'frame', split_axis=0, concat_axis=1, tiled=T...  35.3 us
    slice x1, local copies, waits for them, and re-layouts, on_device(): gathered[:, :, 2].reshape(frames_all, patch_rows, heads_here, HD)  23.3 us
    psum x1, waiting for transfers between devices, on_device(): lax.psum(spatial_part.astype(jnp.bfloat16), 'mp').astype(jnp.float32)  23 us
    sub x2, matrix products, soft_weights(): raised = jnp.exp(scores - row_top)  22.8 us
    psum x1, waiting for transfers between devices, on_device(): lax.psum(temporal_part.astype(jnp.bfloat16), 'mp').astype(jnp.float32)  20.2 us
    dot_general x1, matrix products, on_device(): jnp.einsum('hqk,khd->qhd', weights, spatial_value, preferred_element_type...  12.4 us
  transfers between devices with their start and end apart: 3, of which 3 were waited for; matrix products, arithmetic and copies ran while one was open for 1% of the time, Pallas kernels for 0%

commit v1 on v0

--- a/solution.py
+++ b/solution.py
@@ -1,6 +1,10 @@
+import functools
+
 import jax
 import jax.numpy as jnp
 from jax import lax
+from jax.experimental import pallas as pl
+from jax.experimental.pallas import tpu as pltpu
 from jax.sharding import PartitionSpec as P
 
 HD = 80
@@ -9,6 +13,10 @@
 RCAP = 4
 DEC_HD = 64
 V = 778
+ROWS = 256
+PATCHES = 16
+LOG2E = 1.4426950408889634
+MIB = 1 << 20
 
 
 def layer_norm(values, gain_row):
@@ -37,7 +45,7 @@
     return (live_slots, owner_flat * RCAP + slot_rank)
 
 
-def on_device(
+def on_device_any(
     stream,
     spatial_qkv,
     spatial_out_w,
@@ -117,6 +125,235 @@
     crop_norm = layer_norm(crop_rows.astype(jnp.float32), decoder_gain).reshape(
         MAXC * TILE, model_width
     )
+    return decode(
+        crop_norm, decoder_kv_w, vertex_queries, crop_counts, crop_owner
+    ), stream_part
+
+
+def head_window(head):
+    first = head * HD // 128 * 128
+    last = -(-(head + 1) * HD // 128) * 128
+    return first, last - first, head * HD - first
+
+
+def head_attention(query, key_of, value_of, out_ref, row_slice, heads_here, keep):
+    factor = HD ** (-0.5) * LOG2E
+    done = {}
+    for head in range(heads_here):
+        first, width, start = head_window(head)
+        lane = lax.broadcasted_iota(jnp.int32, (1, width), 1)
+        inside = (lane >= start) & (lane < start + HD)
+        q_here = query[:, first : first + width]
+        q_here = jnp.where(inside, q_here, jnp.zeros_like(q_here))
+        scores = lax.dot_general(
+            q_here,
+            key_of(first, width),
+            (((1,), (1,)), ((), ())),
+            preferred_element_type=jnp.float32,
+        )
+        if keep is not None:
+            scores = jnp.where(keep, scores, -jnp.inf)
+        top = jnp.max(scores, axis=-1, keepdims=True)
+        raised = jnp.exp2(scores * factor - top * factor).astype(jnp.bfloat16)
+        v_here = value_of(first, width)
+        v_here = jnp.where(inside, v_here, jnp.ones_like(v_here))
+        both = jnp.dot(raised, v_here, preferred_element_type=jnp.float32)
+        at = 0 if start else width - 1
+        found = (both / both[:, at : at + 1]).astype(jnp.bfloat16)
+        for tile in range(width // 128):
+            column = first + tile * 128
+            part = found[:, tile * 128 : tile * 128 + 128]
+            if column in done:
+                part = jnp.where(inside[:, tile * 128 : tile * 128 + 128], part, done[column])
+            done[column] = part
+    for column, part in done.items():
+        out_ref[row_slice, column : column + 128] = part
+
+
+def spatial_kernel(q_ref, k_ref, v_ref, w_ref, mine_ref, other_ref, heads_ref):
+    here = lax.axis_index("mp")
+    cols = q_ref.shape[1]
+    head_attention(
+        q_ref[...],
+        lambda first, width: k_ref[:, first : first + width],
+        lambda first, width: v_ref[:, first : first + width],
+        heads_ref,
+        slice(None),
+        cols // HD,
+        None,
+    )
+    half = mine_ref.shape[1]
+    for out_ref, group in ((mine_ref, here), (other_ref, 1 - here)):
+        columns = pl.ds(pl.multiple_of(group * half, 128), half)
+        out_ref[...] = jnp.dot(
+            heads_ref[...], w_ref[:, columns], preferred_element_type=jnp.float32
+        ).astype(jnp.bfloat16)
+
+
+def spatial_attention(query, key, value, weight):
+    patches, cols = query.shape
+    half = weight.shape[1] // 2
+    whole = lambda i: (0, 0)
+    block = lambda i: (i, 0)
+    return pl.pallas_call(
+        spatial_kernel,
+        grid=(patches // ROWS,),
+        in_specs=[
+            pl.BlockSpec((ROWS, cols), block),
+            pl.BlockSpec((patches, cols), whole),
+            pl.BlockSpec((patches, cols), whole),
+            pl.BlockSpec(weight.shape, whole),
+        ],
+        out_specs=[pl.BlockSpec((ROWS, half), block)] * 2,
+        out_shape=[jax.ShapeDtypeStruct((patches, half), jnp.bfloat16)] * 2,
+        scratch_shapes=[pltpu.VMEM((ROWS, cols), jnp.bfloat16)],
+        compiler_params=pltpu.CompilerParams(vmem_limit_bytes=48 * MIB),
+        name="spatial",
+    )(query, key, value, weight)
+
+
+def temporal_kernel(
+    mid_mine, mid_other, gain_ref, w_ref, out_w_ref, mine_ref, other_ref, qkv_ref, heads_ref
+):
+    here = lax.axis_index("mp")
+    frames_all, rows, half = mid_mine.shape
+    total = frames_all * rows
+    model = 2 * half
+    pair = [
+        (ref[...].reshape(total, half).astype(jnp.float32), pl.multiple_of(group * half, 128))
+        for ref, group in ((mid_mine, here), (mid_other, 1 - here))
+    ]
+    mean = sum(jnp.sum(part, axis=-1, keepdims=True) for part, _ in pair) / model
+    pair = [(part - mean, first) for part, first in pair]
+    spread = sum(jnp.sum(part * part, axis=-1, keepdims=True) for part, _ in pair) / model
+    scale = lax.rsqrt(spread + 1e-06)
+    pair = [
+        (
+            (part * scale * gain_ref[:, pl.ds(first, half)].astype(jnp.float32)).astype(
+                jnp.bfloat16
+            ),
+            first,
+        )
+        for part, first in pair
+    ]
+    for which in range(3):
+        qkv_ref[which] = sum(
+            jnp.dot(part, w_ref[which, pl.ds(first, half), :], preferred_element_type=jnp.float32)
+            for part, first in pair
+        ).astype(jnp.bfloat16)
+    row_patch = lax.broadcasted_iota(jnp.int32, (total, total), 0) % rows
+    col_patch = lax.broadcasted_iota(jnp.int32, (total, total), 1) % rows
+    cols = qkv_ref.shape[2]
+    head_attention(
+        qkv_ref[0],
+        lambda first, width: qkv_ref[1, :, first : first + width],
+        lambda first, width: qkv_ref[2, :, first : first + width],
+        heads_ref,
+        slice(None),
+        cols // HD,
+        row_patch == col_patch,
+    )
+    for out_ref, group in ((mine_ref, here), (other_ref, 1 - here)):
+        columns = pl.ds(pl.multiple_of(group * half, 128), half)
+        out_ref[...] = (
+            jnp.dot(heads_ref[...], out_w_ref[:, columns], preferred_element_type=jnp.float32)
+            .astype(jnp.bfloat16)
+            .reshape(frames_all, rows, half)
+        )
+
+
+def temporal_attention(mid_mine, mid_other, gain, weights, out_weight):
+    frames_all, patch_rows, half = mid_mine.shape
+    cols = weights.shape[2]
+    total = frames_all * PATCHES
+    block = pl.BlockSpec((frames_all, PATCHES, half), lambda i: (0, i, 0))
+    return pl.pallas_call(
+        temporal_kernel,
+        grid=(patch_rows // PATCHES,),
+        in_specs=[
+            block,
+            block,
+            pl.BlockSpec((1, 2 * half), lambda i: (0, 0)),
+            pl.BlockSpec(weights.shape, lambda i: (0, 0, 0)),
+            pl.BlockSpec(out_weight.shape, lambda i: (0, 0)),
+        ],
+        out_specs=[block, block],
+        out_shape=[jax.ShapeDtypeStruct(mid_mine.shape, jnp.bfloat16)] * 2,
+        scratch_shapes=[
+            pltpu.VMEM((3, total, cols), jnp.bfloat16),
+            pltpu.VMEM((total, cols), jnp.bfloat16),
+        ],
+        compiler_params=pltpu.CompilerParams(vmem_limit_bytes=48 * MIB),
+        name="temporal",
+    )(mid_mine, mid_other, gain.reshape(1, -1), weights, out_weight)
+
+
+def swap(values):
+    return lax.ppermute(values, "mp", [(0, 1), (1, 0)])
+
+
+def added(base, mine, other):
+    update = mine.astype(jnp.float32) + other.astype(jnp.float32)
+    return (base.astype(jnp.float32) + update).astype(jnp.bfloat16)
+
+
+def on_device_pair(
+    stream,
+    spatial_qkv,
+    spatial_out_w,
+    temporal_gain,
+    temporal_qkv_w,
+    temporal_out_w,
+    decoder_gain,
+    decoder_kv_w,
+    vertex_queries,
+    crop_counts,
+    crop_tiles,
+    crop_owner,
+):
+    patches = stream.shape[1]
+    half = stream.shape[2] // 2
+    frames_all = crop_owner.shape[0]
+    here = lax.axis_index("mp")
+    mine, theirs = spatial_attention(
+        spatial_qkv[0, :, 0], spatial_qkv[0, :, 1], spatial_qkv[0, :, 2], spatial_out_w
+    )
+    stream_half = lax.dynamic_slice_in_dim(stream[0], here * half, half, 1)
+    middle = added(stream_half, mine, swap(theirs))
+    mid_mine = lax.all_to_all(
+        middle.reshape(frames_all, patches // frames_all, half),
+        "frame",
+        split_axis=0,
+        concat_axis=0,
+        tiled=True,
+    )
+    mid_other = swap(mid_mine)
+    mine, theirs = temporal_attention(
+        mid_mine, mid_other, temporal_gain, temporal_qkv_w, temporal_out_w
+    )
+    final_mine = added(mid_mine, mine, swap(theirs))
+    stream_part = lax.all_to_all(
+        final_mine, "frame", split_axis=0, concat_axis=0, tiled=True
+    ).reshape(1, patches, half)
+    frame_id = lax.axis_index("frame")
+    my_tiles = lax.dynamic_index_in_dim(crop_tiles, frame_id, 0, keepdims=False)
+    tile_view = stream_part.reshape(patches // TILE, TILE, half)
+    crop_mine = jnp.take(tile_view, my_tiles, axis=0).reshape(MAXC * TILE, half)
+    crop_other = swap(crop_mine)
+    crop_rows = jnp.where(
+        here == 0,
+        jnp.concatenate([crop_mine, crop_other], axis=1),
+        jnp.concatenate([crop_other, crop_mine], axis=1),
+    )
+    crop_norm = layer_norm(crop_rows.astype(jnp.float32), decoder_gain)
+    return decode(
+        crop_norm, decoder_kv_w, vertex_queries, crop_counts, crop_owner
+    ), stream_part
+
+
+def decode(crop_norm, decoder_kv_w, vertex_queries, crop_counts, crop_owner):
+    frame_id = lax.axis_index("frame")
+    frames_all = crop_owner.shape[0]
     dec_local = decoder_kv_w.shape[2]
     crop_keys = jnp.dot(crop_norm, decoder_kv_w[0], preferred_element_type=jnp.float32).astype(
         jnp.bfloat16
@@ -155,7 +392,7 @@
     decoded = jnp.einsum(
         "rhvt,rthd->rhdv", vertex_weights, slot_values, preferred_element_type=jnp.float32
     )
-    return (decoded.astype(jnp.bfloat16).reshape(RCAP, dec_local, V), stream_part)
+    return decoded.astype(jnp.bfloat16).reshape(RCAP, dec_local, V)
 
 
 def solution(mesh):
@@ -174,7 +411,7 @@
         P(),
     )
     return jax.shard_map(
-        on_device,
+        on_device_pair if mesh.shape["mp"] == 2 else on_device_any,
         mesh=mesh,
         in_specs=placed,
         out_specs=(P("frame", "mp", None), P("frame", None, "mp")),

time: 431 us -> 214 us (0.50); the launches traced: 423 us -> 213 us
  blocking collectives: 157 us -> 37.1 us
  local copies, waits for them, and re-layouts: 70.5 us -> 14.7 us
  matrix products: 67.7 us -> 12.7 us
  Pallas kernels: 0 us -> 43.2 us
  between operations: 14.8 us -> 0.87 us
  other arithmetic: 15.5 us -> 5.88 us
    all_to_all x2 -> x1, blocking collectives: 157 us -> 37.1 us  [on_device_pair(): lax.all_to_all(middle.reshape(frames_all, patches // frames_all, half), '...]
    psum x2 -> x0, waiting for transfers between devices: 43.2 us -> none  [the longest x1 23 us: on_device(): lax.psum(spatial_part.astype(jnp.bfloat16), 'mp').astype(jnp.float32)]
    pallas_call x0 -> x2, Pallas kernels: none -> 43.2 us  [the longest x1 25.1 us: temporal_attention(): pl.pallas_call(temporal_kernel, grid=(patch_rows // PATCHES,), in_specs=[...]
    dot_general x13 -> x5, matrix products: 45 us -> 7.93 us  [the longest x1 4.18 us: decode(): jnp.einsum('rhvt,rthd->rhdv', vertex_weights, slot_values, preferred_elem...]
    slice x8 -> x3, local copies, waits for them, and re-layouts: 35.1 us -> 0.64 us  [the longest x2 0.41 us: decode(): slot_pairs[:, :, :dec_local].reshape(RCAP, TILE, heads_dec, DEC_HD)]
    all_to_all x1 -> x2, waiting for transfers between devices: 45.8 us -> 76.5 us  [the longest x1 45.3 us: decode(): lax.all_to_all(outgoing, 'frame', split_axis=0, concat_axis=0, tiled=True)]
    sub x2 -> x1, matrix products: 22.8 us -> 4.81 us  [soft_weights(): raised = jnp.exp(scores - row_top)]
    another operation x3 -> x0, local copies, waits for them, and re-layouts: 14.1 us -> none  [the longest x1 4.84 us: on_device(): gathered[:, :, 2].reshape(frames_all, patch_rows, heads_here, HD)]
  transfers between devices with their start and end apart: 3 -> 6, of which waited for: 3 -> 6; matrix products, arithmetic and copies ran while one was open for 1% -> 2% of each run, Pallas kernels for 0% -> 0%
where the time goes in v1:
time: 214 us; the launch traced here: 213 us
  waiting for transfers between devices  86.1 us (40%)
  Pallas kernels  43.2 us (20%)
  blocking collectives  37.1 us (17%)
  local copies, waits for them, and re-layouts  14.7 us (7%)
  matrix products  12.7 us (6%)
  starting transfers between devices  12.2 us (6%)
  other arithmetic  5.88 us (3%)
    all_to_all x1, waiting for transfers between devices, decode(): lax.all_to_all(outgoing, 'frame', split_axis=0, concat_axis=0, tiled=True)  45.3 us
    all_to_all x1, blocking collectives, on_device_pair(): lax.all_to_all(middle.reshape(frames_all, patches // frames_all, half), '...  37.1 us
    all_to_all x1, waiting for transfers between devices, on_device_pair(): lax.all_to_all(final_mine, 'frame', split_axis=0, concat_axis=0, tiled=True)  31.3 us
    pallas_call x1, Pallas kernels, temporal_attention(): pl.pallas_call(temporal_kernel, grid=(patch_rows // PATCHES,), in_specs=[...  25.1 us
    pallas_call x1, Pallas kernels, spatial_attention(): pl.pallas_call(spatial_kernel, grid=(patches // ROWS,), in_specs=[pl.Bloc...  18.1 us
    ppermute x4, waiting for transfers between devices, swap(): return lax.ppermute(values, 'mp', [(0, 1), (1, 0)])  9.61 us
    all_to_all x1, starting transfers between devices, on_device_pair(): lax.all_to_all(final_mine, 'frame', split_axis=0, concat_axis=0, tiled=True)  6.41 us
    unnamed x18, local copies, waits for them, and re-layouts  5.9 us
  transfers between devices with their start and end apart: 6, of which 6 were waited for; matrix products, arithmetic and copies ran while one was open for 2% of the time, Pallas kernels for 0%

profile of v1, /device:TPU:14, one launch (start us, length us, event | category | flops | bytes accessed | tf_op | source)
XLA Modules:
  0.0 212.9 jit_solution(1011622025217106119)
XLA Ops:
  0.6 3.5 %slice_bitcast_fusion = (bf16[1024,640]{1,0:T(8,128)(2,1)}, bf16[1024,640]{1,0:T(8,128)(2,1)S(1)}, bf16[1024,640]{1,0:T(8,128)(2,1)S(1)}) fusion(bf16[1,1024,3,640]{3,1,2,0:T(8,128)(2,1)} %param.13), kind=kLoop, calls=%fused_computation.25 | loop fusion | bytes 7864320 | tf_op jit(solution)/shard_map/squeeze | solution.py:319
  4.1 18.1 %spatial.1 = (bf16[1024,640]{1,0:T(8,128)(2,1)S(1)}, bf16[1024,640]{1,0:T(8,128)(2,1)S(1)}) custom-call(bf16[1024,640]{1,0:T(8,128)(2,1)S(1)} %get-tuple-element.21.q_ref, bf16[1024,640]{1,0:T(8,128)(2,1)S(1)} %get-tuple-element.22.k_ref, bf16[1024,640]{1,0:T(8,128)(2,1)} %get-tuple-element.20.v_ref, bf16[640,1280]{1,0:T(8,128)(2,1)} %w_ref.2), custom_call_target="tpu_custom_call" | custom-call | tf_op jit(solution)/shard_map/spatial/pallas_call | solution.py:198
  22.3 0.1 collective-permute-start
  22.4 3.1 %collective-permute-done = bf16[1024,640]{1,0:T(8,128)(2,1)} collective-permute-done((bf16[1024,640]{1,0:T(8,128)(2,1)S(1)}, bf16[1024,640]{1,0:T(8,128)(2,1)}, u32[]{:S(2)}, u32[]{:S(2)}) %collective-permute-start) | collective-permute-done | bytes 1310752 | tf_op jit(solution)/shard_map/ppermute | solution.py:292
  25.5 2.2 %fusion.9 = bf16[1024,640]{1,0:T(8,128)(2,1)S(1)} fusion(bf16[1024,640]{1,0:T(8,128)(2,1)} %collective-permute-done, bf16[1024,640]{1,0:T(8,128)(2,1)S(1)} %get-tuple-element.6, bf16[1,1024,1280]{2,1,0:T(8,128)(2,1)} %param.12, s32[]{:T(128)S(6)} %select_n.42), kind=kLoop, calls=%fused_computation.12 | loop fusion | flops 3932160 | bytes 5242884 | tf_op jit(solution)/shard_map/convert_element_type | solution.py:297
  27.7 0.0 copy-start.3
  27.7 37.1 %all_to_all.15.mid_mine = bf16[16,64,640]{2,1,0:T(8,128)(2,1)S(1)} all-to-all(bf16[16,64,640]{2,1,0:T(8,128)(2,1)S(1)} %bitcast.58), channel_id=1, replica_groups=mesh['frame'=16,'mp'=2] {'frame'}, dimensions={0} | all-to-all | bytes 2621440 | tf_op jit(solution)/shard_map/all_to_all | solution.py:323
  64.8 0.0 collective-permute-start.1
  64.8 0.0 copy-done.3
  64.8 3.0 %collective-permute-done.1.mid_other = bf16[16,64,640]{2,1,0:T(8,128)(2,1)S(1)} collective-permute-done((bf16[16,64,640]{2,1,0:T(8,128)(2,1)S(1)}, bf16[16,64,640]{2,1,0:T(8,128)(2,1)S(1)}, u32[]{:S(2)}, u32[]{:S(2)}) %collective-permute-start.1) | collective-permute-done | bytes 1310752 | tf_op jit(solution)/shard_map/ppermute | solution.py:292
  67.9 25.1 %temporal.1 = (bf16[16,64,640]{2,1,0:T(8,128)(2,1)S(1)}, bf16[16,64,640]{2,1,0:T(8,128)(2,1)S(1)}) custom-call(bf16[16,64,640]{2,1,0:T(8,128)(2,1)S(1)} %all_to_all.15.mid_mine, bf16[16,64,640]{2,1,0:T(8,128)(2,1)S(1)} %collective-permute-done.1.mid_other, bf16[1,1280]{1,0:T(2,128)(2,1)S(1)} %reshape.144.gain_ref, bf16[3,1280,640]{2,1,0:T(8,128)(2,1)} %w_ref.3, ...), custom_call_target="tpu_custom_call" | custom-call | tf_op jit(solution)/shard_map/temporal/pallas_call | solution.py:270
  93.0 0.2 collective-permute-start.2
  93.2 2.9 %collective-permute-done.2 = bf16[16,64,640]{2,1,0:T(8,128)(2,1)S(1)} collective-permute-done((bf16[16,64,640]{2,1,0:T(8,128)(2,1)S(1)}, bf16[16,64,640]{2,1,0:T(8,128)(2,1)S(1)}, u32[]{:S(2)}, u32[]{:S(2)}) %collective-permute-start.2) | collective-permute-done | bytes 1310752 | tf_op jit(solution)/shard_map/ppermute | solution.py:292
  96.1 1.6 add_convert_fusion
  97.7 0.0 copy-start.1
  97.7 0.0 copy-start.4
  97.7 0.0 copy-start.5
  97.7 0.0 copy-start.2
  97.7 6.4 %all-to-all-start.1 = ((bf16[16,64,640]{2,1,0:T(8,128)(2,1)}), bf16[16,64,640]{2,1,0:T(8,128)(2,1)S(1)}, u32[]{:S(2)}, u32[]{:S(2)}) async-start(bf16[16,64,640]{2,1,0:T(8,128)(2,1)} %add_convert_fusion), calls=%async_computation.1 | async-start | bytes 2621440 | tf_op jit(solution)/shard_map/all_to_all | solution.py:335
  104.1 0.0 copy-done.1
  104.1 0.0 copy-done.4
  104.1 0.2 dynamic-slice_reduce_fusion
  104.4 0.1 broadcast_bitcast_fusion
  104.5 31.3 %all-to-all-done.1 = bf16[16,64,640]{2,1,0:T(8,128)(2,1)S(1)} async-done(((bf16[16,64,640]{2,1,0:T(8,128)(2,1)}), bf16[16,64,640]{2,1,0:T(8,128)(2,1)S(1)}, u32[]{:S(2)}, u32[]{:S(2)}) %all-to-all-start.1) | async-done | bytes 1310752 | tf_op jit(solution)/shard_map/all_to_all | solution.py:335
  135.7 0.6 gather_fusion
  136.4 0.1 bitcast_select_fusion
  136.5 0.1 collective-permute-start.3
  136.6 0.0 copy-done.5
  136.6 0.0 copy-start.6
  136.6 0.6 dynamic_slice.15
  137.2 0.0 copy-done.2
  137.2 0.6 iota_compare_fusion.3
  137.9 0.6 collective-permute-done.3
  138.4 0.3 convert_reduce_fusion
  138.7 0.4 fusion.14
  139.1 0.0 copy-done.6
  139.1 0.8 convolution_convert_fusion.1
  139.9 0.8 convolution_convert_fusion.2
  140.8 0.2 copy.59
  141.0 0.9 convolution_convert_fusion
  141.9 2.5 %copy.61 = bf16[16,128,512]{2,1,0:T(8,128)(2,1)} copy(bf16[16,128,512]{2,0,1:T(8,128)(2,1)S(1)} %convolution_convert_fusion) | data formatting | bytes 4194304 | tf_op jit(solution)/shard_map/convert_element_type | solution.py:378
  144.4 5.5 %all-to-all-start.2 = ((bf16[16,128,512]{2,1,0:T(8,128)(2,1)}), bf16[16,128,512]{2,1,0:T(8,128)(2,1)S(1)}, u32[]{:S(2)}, u32[]{:S(2)}) async-start(bf16[16,128,512]{2,1,0:T(8,128)(2,1)} %copy.61), calls=%async_computation.2 | async-start | bytes 4194304 | tf_op jit(solution)/shard_map/all_to_all | solution.py:379
  149.8 0.1 iota_compare_fusion.1
  149.9 0.1 lt.62
  150.0 0.1 copy.58
  150.1 0.1 copy.56
  150.2 0.1 eq.47
  150.3 0.1 fusion.38
  150.4 0.1 reduce_window_sum.11
  150.5 0.2 select_reduce_fusion
  150.6 0.1 reduce_sum.48
  150.7 0.1 copy.57
  150.8 2.0 copy.65
  152.8 0.1 convert_reduce_fusion.1
  152.9 45.3 %all-to-all-done.2 = bf16[16,128,512]{2,1,0:T(8,128)(2,1)S(1)} async-done(((bf16[16,128,512]{2,1,0:T(8,128)(2,1)}), bf16[16,128,512]{2,1,0:T(8,128)(2,1)S(1)}, u32[]{:S(2)}, u32[]{:S(2)}) %all-to-all-start.2) | async-done | bytes 2097184 | tf_op jit(solution)/shard_map/all_to_all | solution.py:379
  198.1 1.3 fusion.20
  199.5 0.2 fusion.50
  199.6 0.2 copy.64
  199.9 0.2 copy.63
  200.1 0.4 copy-done
  200.5 4.8 %fusion.51 = (f32[4,4,778]{2,0,1:T(4,128)S(1)}, f32[4,4,778,128]{3,2,0,1:T(8,128)}) fusion(bf16[778,4,64,1]{0,2,3,1:T(8,128)(2,1)S(1)} %bitcast.61, bf16[4,128,4,64]{1,3,2,0:T(8,128)(2,1)S(1)} %bitcast.62), kind=kOutput, calls=%fused_computation.71 | convolution fusion | flops 208728192 | bytes 7083648 | tf_op jit(solution)/shard_map/sub | solution.py:31
  205.3 4.2 %fusion.17 = bf16[4,4,64,778]{3,2,1,0:T(8,128)(2,1)S(1)} fusion(bf16[4,128,4,64]{1,3,2,0:T(8,128)(2,1)S(1)} %bitcast.63, f32[4,4,778,128]{3,2,0,1:T(8,128)} %get-tuple-element.26, f32[4,4,778]{2,0,1:T(4,128)S(1)} %get-tuple-element.25), kind=kOutput, calls=%fused_computation.24 | convolution fusion | flops 207931392 | bytes 8278656 | tf_op jit(solution)/shard_map/rhvt,rthd->rhdv/dot_general | solution.py:392
  209.5 2.4 %copy.68 = bf16[4,256,778]{1,0,2:T(4,128)(2,1)} copy(bf16[4,256,778]{2,1,0:T(8,128)(2,1)S(1)} %bitcast.60) | data formatting | bytes 3186688
  211.9 1.1 copy.93
  (11 shorter events, 0.1 us)
Async XLA Ops:
  22.3 3.2 %collective-permute-start = (bf16[1024,640]{1,0:T(8,128)(2,1)S(1)}, bf16[1024,640]{1,0:T(8,128)(2,1)}, u32[]{:S(2)}, u32[]{:S(2)}) collective-permute-start(bf16[1024,640]{1,0:T(8,128)(2,1)S(1)} %get-tuple-element.7), channel_id=1, source_target_pairs={{0,1},{1,0},{2,3},{3,2},{4,5},{5,4},{6,7},{7,6},{8,9},{9,8},{10,11... | collective-permute-start | bytes 3932168 | tf_op jit(solution)/shard_map/ppermute | solution.py:292
  27.7 37.1 %copy-start.3 = (bf16[1280]{0:T(1024)(128)(2,1)S(1)}, bf16[1280]{0:T(1024)(128)(2,1)}, u32[]{:S(2)}) copy-start(bf16[1280]{0:T(1024)(128)(2,1)} %param.15) | copy-start | bytes 7684
  64.8 3.0 %collective-permute-start.1 = (bf16[16,64,640]{2,1,0:T(8,128)(2,1)S(1)}, bf16[16,64,640]{2,1,0:T(8,128)(2,1)S(1)}, u32[]{:S(2)}, u32[]{:S(2)}) collective-permute-start(bf16[16,64,640]{2,1,0:T(8,128)(2,1)S(1)} %all_to_all.15.mid_mine), channel_id=1, source_target_pairs={{0,1},{1,0},{2,3},{3,2},{4,5},{5,4},{6,7},{7,6},{8,9},{9,8},{10,11... | collective-permute-start | bytes 3932168 | tf_op jit(solution)/shard_map/ppermute | solution.py:292
  93.0 3.1 %collective-permute-start.2 = (bf16[16,64,640]{2,1,0:T(8,128)(2,1)S(1)}, bf16[16,64,640]{2,1,0:T(8,128)(2,1)S(1)}, u32[]{:S(2)}, u32[]{:S(2)}) collective-permute-start(bf16[16,64,640]{2,1,0:T(8,128)(2,1)S(1)} %get-tuple-element.9), channel_id=1, source_target_pairs={{0,1},{1,0},{2,3},{3,2},{4,5},{5,4},{6,7},{7,6},{8,9},{9,8},{10,11... | collective-permute-start | bytes 3932168 | tf_op jit(solution)/shard_map/ppermute | solution.py:292
  97.7 6.4 %copy-start.1 = (s32[16,3]{0,1:T(4,128)S(1)}, s32[16,3]{0,1:T(4,128)}, u32[]{:S(2)}) copy-start(s32[16,3]{0,1:T(4,128)} %param.23) | copy-start | bytes 580
  97.7 6.4 %copy-start.4 = (s32[16,3]{0,1:T(4,128)S(1)}, s32[16,3]{0,1:T(4,128)}, u32[]{:S(2)}) copy-start(s32[16,3]{0,1:T(4,128)} %param.22) | copy-start | bytes 580
  97.7 38.9 %copy-start.5 = (s32[16]{0:T(128)S(1)}, s32[16]{0:T(128)}, u32[]{:S(2)}) copy-start(s32[16]{0:T(128)} %param.21) | copy-start | bytes 196
  97.7 39.5 %copy-start.2 = (bf16[1280]{0:T(1024)(128)(2,1)S(1)}, bf16[1280]{0:T(1024)(128)(2,1)}, u32[]{:S(2)}) copy-start(bf16[1280]{0:T(1024)(128)(2,1)} %param.18) | copy-start | bytes 7684
  97.7 38.0 %all-to-all-start.1 = ((bf16[16,64,640]{2,1,0:T(8,128)(2,1)}), bf16[16,64,640]{2,1,0:T(8,128)(2,1)S(1)}, u32[]{:S(2)}, u32[]{:S(2)}) async-start(bf16[16,64,640]{2,1,0:T(8,128)(2,1)} %add_convert_fusion), calls=%async_computation.1 | async-start | bytes 2621440 | tf_op jit(solution)/shard_map/all_to_all | solution.py:335
  136.5 1.9 collective-permute-start.3
  136.6 2.5 %copy-start.6 = (bf16[2,1280,256]{2,1,0:T(8,128)(2,1)S(1)}, bf16[2,1280,256]{2,1,0:T(8,128)(2,1)}, u32[]{:S(2)}) copy-start(bf16[2,1280,256]{2,1,0:T(8,128)(2,1)} %param.19) | copy-start | bytes 3932164
  144.4 53.8 %all-to-all-start.2 = ((bf16[16,128,512]{2,1,0:T(8,128)(2,1)}), bf16[16,128,512]{2,1,0:T(8,128)(2,1)S(1)}, u32[]{:S(2)}, u32[]{:S(2)}) async-start(bf16[16,128,512]{2,1,0:T(8,128)(2,1)} %copy.61), calls=%async_computation.2 | async-start | bytes 4194304 | tf_op jit(solution)/shard_map/all_to_all | solution.py:379
  199.4 1.0 copy-start

commit v2 on v1

--- a/solution.py
+++ b/solution.py
@@ -15,6 +15,7 @@
 V = 778
 ROWS = 256
 PATCHES = 16
+CHUNKS = 2
 LOG2E = 1.4426950408889634
 MIB = 1 << 20
 
@@ -200,8 +201,8 @@
         grid=(patches // ROWS,),
         in_specs=[
             pl.BlockSpec((ROWS, cols), block),
-            pl.BlockSpec((patches, cols), whole),
-            pl.BlockSpec((patches, cols), whole),
+            pl.BlockSpec(key.shape, whole),
+            pl.BlockSpec(key.shape, whole),
             pl.BlockSpec(weight.shape, whole),
         ],
         out_specs=[pl.BlockSpec((ROWS, half), block)] * 2,
@@ -315,26 +316,40 @@
     half = stream.shape[2] // 2
     frames_all = crop_owner.shape[0]
     here = lax.axis_index("mp")
-    mine, theirs = spatial_attention(
-        spatial_qkv[0, :, 0], spatial_qkv[0, :, 1], spatial_qkv[0, :, 2], spatial_out_w
-    )
+    own_rows = patches // frames_all
+    part_rows = own_rows // CHUNKS
+
+    def chunk_of(values, chunk):
+        split = values.reshape(frames_all, CHUNKS, part_rows, values.shape[1])
+        return split[:, chunk].reshape(frames_all * part_rows, values.shape[1])
+
+    key, value = spatial_qkv[0, :, 1], spatial_qkv[0, :, 2]
     stream_half = lax.dynamic_slice_in_dim(stream[0], here * half, half, 1)
-    middle = added(stream_half, mine, swap(theirs))
-    mid_mine = lax.all_to_all(
-        middle.reshape(frames_all, patches // frames_all, half),
-        "frame",
-        split_axis=0,
-        concat_axis=0,
-        tiled=True,
-    )
-    mid_other = swap(mid_mine)
-    mine, theirs = temporal_attention(
-        mid_mine, mid_other, temporal_gain, temporal_qkv_w, temporal_out_w
-    )
-    final_mine = added(mid_mine, mine, swap(theirs))
-    stream_part = lax.all_to_all(
-        final_mine, "frame", split_axis=0, concat_axis=0, tiled=True
-    ).reshape(1, patches, half)
+    arrived = []
+    for chunk in range(CHUNKS):
+        mine, theirs = spatial_attention(
+            chunk_of(spatial_qkv[0, :, 0], chunk), key, value, spatial_out_w
+        )
+        middle = added(chunk_of(stream_half, chunk), mine, swap(theirs))
+        arrived.append(
+            lax.all_to_all(
+                middle.reshape(frames_all, part_rows, half),
+                "frame",
+                split_axis=0,
+                concat_axis=0,
+                tiled=True,
+            )
+        )
+    returned = []
+    for mid_mine in arrived:
+        mine, theirs = temporal_attention(
+            mid_mine, swap(mid_mine), temporal_gain, temporal_qkv_w, temporal_out_w
+        )
+        final_mine = added(mid_mine, mine, swap(theirs))
+        returned.append(
+            lax.all_to_all(final_mine, "frame", split_axis=0, concat_axis=0, tiled=True)
+        )
+    stream_part = jnp.stack(returned, axis=1).reshape(1, patches, half)
     frame_id = lax.axis_index("frame")
     my_tiles = lax.dynamic_index_in_dim(crop_tiles, frame_id, 0, keepdims=False)
     tile_view = stream_part.reshape(patches // TILE, TILE, half)
@@ -381,6 +396,8 @@
     slot_pairs = jnp.einsum(
         "rg,gtc->rtc", by_frame, incoming, preferred_element_type=jnp.float32
     ).astype(jnp.bfloat16)
+    if dec_local % 128 == 0:
+        return vertex_decoder(slot_pairs, vertex_queries)
     heads_dec = dec_local // DEC_HD
     slot_keys = slot_pairs[:, :, :dec_local].reshape(RCAP, TILE, heads_dec, DEC_HD)
     slot_values = slot_pairs[:, :, dec_local:].reshape(RCAP, TILE, heads_dec, DEC_HD)
@@ -393,6 +410,48 @@
         "rhvt,rthd->rhdv", vertex_weights, slot_values, preferred_element_type=jnp.float32
     )
     return decoded.astype(jnp.bfloat16).reshape(RCAP, dec_local, V)
+
+
+def decoder_kernel(pair_ref, query_ref, out_ref):
+    width = query_ref.shape[1]
+    factor = DEC_HD ** (-0.5) * LOG2E
+    values = pair_ref[0, :, width:].T
+    lane = lax.broadcasted_iota(jnp.int32, (1, 128), 1)
+    for head in range(width // DEC_HD):
+        start = head * DEC_HD
+        first = start // 128 * 128
+        inside = (lane >= start - first) & (lane < start - first + DEC_HD)
+        keys = pair_ref[0, :, first : first + 128]
+        keys = jnp.where(inside, keys, jnp.zeros_like(keys))
+        scores = lax.dot_general(
+            keys,
+            query_ref[:, first : first + 128],
+            (((1,), (1,)), ((), ())),
+            preferred_element_type=jnp.float32,
+        )
+        top = jnp.max(scores, axis=0, keepdims=True)
+        raised = jnp.exp2((scores - top) * factor)
+        weights = (raised / jnp.sum(raised, axis=0, keepdims=True)).astype(jnp.bfloat16)
+        out_ref[0, start : start + DEC_HD, :] = jnp.dot(
+            values[start : start + DEC_HD], weights, preferred_element_type=jnp.float32
+        ).astype(jnp.bfloat16)
+
+
+def vertex_decoder(slot_pairs, queries):
+    slots, keys, both = slot_pairs.shape
+    vertices, width = queries.shape
+    return pl.pallas_call(
+        decoder_kernel,
+        grid=(slots,),
+        in_specs=[
+            pl.BlockSpec((1, keys, both), lambda i: (i, 0, 0)),
+            pl.BlockSpec((vertices, width), lambda i: (0, 0)),
+        ],
+        out_specs=pl.BlockSpec((1, width, vertices), lambda i: (i, 0, 0)),
+        out_shape=jax.ShapeDtypeStruct((slots, width, vertices), jnp.bfloat16),
+        compiler_params=pltpu.CompilerParams(vmem_limit_bytes=32 * MIB),
+        name="decoder",
+    )(slot_pairs, queries)
 
 
 def solution(mesh):

time: 214 us -> 210 us (0.981)
  blocking collectives: 37.1 us -> 0 us
  starting transfers between devices: 12.2 us -> 34.8 us
  waiting for transfers between devices: 86.1 us -> 71.5 us
  local copies, waits for them, and re-layouts: 14.7 us -> 28.5 us
  other arithmetic: 5.88 us -> 14.7 us
  Pallas kernels: 43.2 us -> 50.6 us
  matrix products: 12.7 us -> 7.82 us
    all_to_all x1 -> x0, blocking collectives: 37.1 us -> none  [on_device_pair(): lax.all_to_all(middle.reshape(frames_all, patches // frames_all, half), '...]
    all_to_all x1 -> x2, waiting for transfers between devices: 31.3 us -> 15.9 us  [on_device_pair(): lax.all_to_all(final_mine, 'frame', split_axis=0, concat_axis=0, tiled=True)]
    all_to_all x0 -> x2, starting transfers between devices: none -> 14.1 us  [on_device_pair(): lax.all_to_all(middle.reshape(frames_all, part_rows, half), 'frame', spli...]
    unnamed x18 -> x42, local copies, waits for them, and re-layouts: 5.9 us -> 15.8 us
    all_to_all x1 -> x2, starting transfers between devices: 6.41 us -> 13.8 us  [on_device_pair(): lax.all_to_all(final_mine, 'frame', split_axis=0, concat_axis=0, tiled=True)]
    pallas_call x0 -> x1, Pallas kernels: none -> 5.78 us  [vertex_decoder(): pl.pallas_call(decoder_kernel, grid=(slots,), in_specs=[pl.BlockSpec((1,...]
    sub x1 -> x0, matrix products: 4.81 us -> none  [soft_weights(): raised = jnp.exp(scores - row_top)]
    dot_general x1 -> x0, matrix products: 4.18 us -> none  [decode(): jnp.einsum('rhvt,rthd->rhdv', vertex_weights, slot_values, preferred_elem...]
  transfers between devices with their start and end apart: 6 -> 12, of which waited for: 6 -> 7; matrix products, arithmetic and copies ran while one was open for 2% -> 4% of each run, Pallas kernels for 0% -> 17%
where the time goes in v2:
time: 210 us; the launch traced here: 209 us
  waiting for transfers between devices  71.5 us (34%)
  Pallas kernels  50.6 us (24%)
  starting transfers between devices  34.8 us (17%)
  local copies, waits for them, and re-layouts  28.5 us (14%)
  other arithmetic  14.7 us (7%)
  matrix products  7.82 us (4%)
    all_to_all x1, waiting for transfers between devices, decode(): lax.all_to_all(outgoing, 'frame', split_axis=0, concat_axis=0, tiled=True)  47.5 us
    pallas_call x2, Pallas kernels, temporal_attention(): pl.pallas_call(temporal_kernel, grid=(patch_rows // PATCHES,), in_specs=[...  27.8 us
    pallas_call x2, Pallas kernels, spatial_attention(): pl.pallas_call(spatial_kernel, grid=(patches // ROWS,), in_specs=[pl.Bloc...  17.1 us
    all_to_all x2, waiting for transfers between devices, on_device_pair(): lax.all_to_all(final_mine, 'frame', split_axis=0, concat_axis=0, tiled=True)  15.9 us
    unnamed x42, local copies, waits for them, and re-layouts  15.8 us
    all_to_all x2, starting transfers between devices, on_device_pair(): lax.all_to_all(middle.reshape(frames_all, part_rows, half), 'frame', spli...  14.1 us
    all_to_all x2, starting transfers between devices, on_device_pair(): lax.all_to_all(final_mine, 'frame', split_axis=0, concat_axis=0, tiled=True)  13.8 us
    ppermute x7, waiting for transfers between devices, swap(): return lax.ppermute(values, 'mp', [(0, 1), (1, 0)])  8.11 us
  transfers between devices with their start and end apart: 12, of which 7 were waited for; matrix products, arithmetic and copies ran while one was open for 4% of the time, Pallas kernels for 17%

profile of v2, /device:TPU:14, one launch (start us, length us, event | category | flops | bytes accessed | tf_op | source)
XLA Modules:
  0.0 209.0 jit_solution(7368422456972963925)
XLA Ops:
  0.6 2.6 %slice_bitcast_fusion = (bf16[1024,640]{1,0:T(8,128)(2,1)S(1)}, bf16[1,1024,1,640]{3,1,2,0:T(8,128)(2,1)S(1)}, bf16[1024,640]{1,0:T(8,128)(2,1)S(1)}) fusion(bf16[1,1024,3,640]{3,1,2,0:T(8,128)(2,1)} %param.13), kind=kLoop, calls=%fused_computation.18 | loop fusion | bytes 7864320 | tf_op jit(solution)/shard_map/squeeze | solution.py:326
  3.3 1.0 fusion.27
  4.3 1.6 copy-done.6
  5.9 8.9 %spatial.2 = (bf16[512,640]{1,0:T(8,128)(2,1)S(1)}, bf16[512,640]{1,0:T(8,128)(2,1)}) custom-call(bf16[512,640]{1,0:T(8,128)(2,1)S(1)} %bitcast.47, bf16[1024,640]{1,0:T(8,128)(2,1)S(1)} %get-tuple-element.30.k_ref, bf16[1024,640]{1,0:T(8,128)(2,1)S(1)} %get-tuple-element.28.v_ref, bf16[640,1280]{1,0:T(8,128)(2,1)S(1)} %copy-done.6), custom_call_target="tpu_custom_call" | custom-call | tf_op jit(solution)/shard_map/spatial/pallas_call | solution.py:199
  14.8 0.1 constant_dynamic-slice_fusion
  14.9 1.0 fusion.26
  15.9 1.3 collective-permute-done
  17.2 2.2 %fusion.8 = bf16[512,640]{1,0:T(8,128)(2,1)} fusion(bf16[512,640]{1,0:T(8,128)(2,1)} %collective-permute-done, bf16[512,640]{1,0:T(8,128)(2,1)S(1)} %get-tuple-element.10, bf16[16,1,32,640]{3,2,1,0:T(8,128)(2,1)S(1)} %get-tuple-element.31), kind=kLoop, calls=%fused_computation.15 | loop fusion | flops 1966080 | bytes 2621440 | tf_op jit(solution)/shard_map/convert_element_type | solution.py:298
  19.4 7.1 %all-to-all-start = ((bf16[16,32,640]{2,1,0:T(8,128)(2,1)}), bf16[16,32,640]{2,1,0:T(8,128)(2,1)S(1)}, u32[]{:S(2)}, u32[]{:S(2)}) async-start(bf16[16,32,640]{2,1,0:T(8,128)(2,1)} %bitcast.51), calls=%async_computation | async-start | bytes 1310720 | tf_op jit(solution)/shard_map/all_to_all | solution.py:335
  26.5 1.3 copy-done.2
  27.8 1.3 copy-done.4
  29.2 1.4 copy-done.7
  30.6 1.1 copy-done.10
  31.7 8.2 %spatial.3 = (bf16[512,640]{1,0:T(8,128)(2,1)S(1)}, bf16[512,640]{1,0:T(8,128)(2,1)S(1)}) custom-call(bf16[512,640]{1,0:T(8,128)(2,1)S(1)} %bitcast.46, bf16[1024,640]{1,0:T(8,128)(2,1)S(1)} %copy-done.4, bf16[1024,640]{1,0:T(8,128)(2,1)S(1)} %copy-done.2, bf16[640,1280]{1,0:T(8,128)(2,1)S(1)} %copy-done.7), custom_call_target="tpu_custom_call" | custom-call | tf_op jit(solution)/shard_map/spatial/pallas_call | solution.py:199
  39.9 2.1 collective-permute-done.3
  42.0 1.1 fusion.7
  43.2 0.1 collective-permute-start.1
  43.3 6.9 %all-to-all-start.2 = ((bf16[16,32,640]{2,1,0:T(8,128)(2,1)}), bf16[16,32,640]{2,1,0:T(8,128)(2,1)}, u32[]{:S(2)}, u32[]{:S(2)}) async-start(bf16[16,32,640]{2,1,0:T(8,128)(2,1)} %bitcast.52), calls=%async_computation.2 | async-start | bytes 1310720 | tf_op jit(solution)/shard_map/all_to_all | solution.py:335
  50.3 1.4 copy-done.8
  51.7 14.2 %temporal.2 = (bf16[16,32,640]{2,1,0:T(8,128)(2,1)S(1)}, bf16[16,32,640]{2,1,0:T(8,128)(2,1)}) custom-call(bf16[16,32,640]{2,1,0:T(8,128)(2,1)S(1)} %all-to-all-done.mid_mine, bf16[16,32,640]{2,1,0:T(8,128)(2,1)} %collective-permute-done.1.mid_other, bf16[1,1280]{1,0:T(2,128)(2,1)S(1)} %reshape.142.gain_ref, bf16[3,1280,640]{2,1,0:T(8,128)(2,1)} %w_ref.7, ...), custom_call_target="tpu_custom_call" | custom-call | tf_op jit(solution)/shard_map/temporal/pallas_call | solution.py:271
  65.9 0.8 copy-done.11
  66.7 0.5 collective-permute-start.4
  67.2 1.9 collective-permute-done.2
  69.2 2.4 %add_convert_fusion.1 = bf16[16,32,640]{2,1,0:T(8,128)(2,1)} fusion(bf16[16,32,640]{2,1,0:T(8,128)(2,1)} %collective-permute-done.2, bf16[16,32,640]{2,1,0:T(8,128)(2,1)} %copy-done.11, bf16[16,32,640]{2,1,0:T(8,128)(2,1)S(1)} %all-to-all-done.mid_mine), kind=kLoop, calls=%fused_computation.17 | loop fusion | flops 1966080 | bytes 2621440 | tf_op jit(solution)/shard_map/convert_element_type | solution.py:298
  71.5 6.9 %all-to-all-start.1 = ((bf16[16,32,640]{2,1,0:T(8,128)(2,1)}), bf16[16,32,640]{2,1,0:T(8,128)(2,1)S(1)}, u32[]{:S(2)}, u32[]{:S(2)}) async-start(bf16[16,32,640]{2,1,0:T(8,128)(2,1)} %add_convert_fusion.1), calls=%async_computation.1 | async-start | bytes 1310720 | tf_op jit(solution)/shard_map/all_to_all | solution.py:350
  78.4 1.4 copy-done.9
  79.9 13.6 %temporal.3 = (bf16[16,32,640]{2,1,0:T(8,128)(2,1)S(1)}, bf16[16,32,640]{2,1,0:T(8,128)(2,1)S(1)}) custom-call(bf16[16,32,640]{2,1,0:T(8,128)(2,1)} %all-to-all-done.2.mid_mine, bf16[16,32,640]{2,1,0:T(8,128)(2,1)} %collective-permute-done.4.mid_other, bf16[1,1280]{1,0:T(2,128)(2,1)S(1)} %reshape.142.gain_ref, bf16[3,1280,640]{2,1,0:T(8,128)(2,1)} %w_ref.7, ...), custom_call_target="tpu_custom_call" | custom-call | tf_op jit(solution)/shard_map/temporal/pallas_call | solution.py:271
  93.6 2.1 collective-permute-done.5
  95.6 2.2 %add_convert_fusion = bf16[16,32,640]{2,1,0:T(8,128)(2,1)} fusion(bf16[16,32,640]{2,1,0:T(8,128)(2,1)S(1)} %collective-permute-done.5, bf16[16,32,640]{2,1,0:T(8,128)(2,1)S(1)} %get-tuple-element.16, bf16[16,32,640]{2,1,0:T(8,128)(2,1)} %all-to-all-done.2.mid_mine), kind=kLoop, calls=%fused_computation.16 | loop fusion | flops 1966080 | bytes 2621440 | tf_op jit(solution)/shard_map/convert_element_type | solution.py:298
  97.8 6.9 %all-to-all-start.3 = ((bf16[16,32,640]{2,1,0:T(8,128)(2,1)}), bf16[16,32,640]{2,1,0:T(8,128)(2,1)}, u32[]{:S(2)}, u32[]{:S(2)}) async-start(bf16[16,32,640]{2,1,0:T(8,128)(2,1)} %add_convert_fusion), calls=%async_computation.3 | async-start | bytes 1310720 | tf_op jit(solution)/shard_map/all_to_all | solution.py:350
  104.8 0.2 dynamic-slice_reduce_fusion
  105.0 0.1 broadcast_bitcast_fusion
  105.1 15.9 %all-to-all-done.3 = bf16[16,32,640]{2,1,0:T(8,128)(2,1)} async-done(((bf16[16,32,640]{2,1,0:T(8,128)(2,1)}), bf16[16,32,640]{2,1,0:T(8,128)(2,1)}, u32[]{:S(2)}, u32[]{:S(2)}) %all-to-all-start.3) | async-done | bytes 655392 | tf_op jit(solution)/shard_map/all_to_all | solution.py:350
  121.0 1.2 pad_maximum_fusion
  122.3 1.2 copy.60
  123.5 2.7 %gather_fusion = bf16[3,128,640]{2,1,0:T(8,128)(2,1)} fusion(bf16[8,128,640]{2,1,0:T(8,128)(2,1)} %bitcast.53, s32[1024]{0:T(1024)S(1)} %pad_clamp_fusion), kind=kCustom, calls=%fused_computation | custom fusion | bytes 983052 | tf_op jit(solution)/shard_map/jit(_take)/gather | solution.py:356
  126.2 1.2 bitcast_select_fusion
  127.5 0.6 dynamic_slice.15
  128.1 0.6 iota_compare_fusion.3
  128.8 0.7 collective-permute-done.6
  129.4 1.5 convert_reduce_fusion
  131.0 1.7 fusion.4
  132.7 2.0 convolution_convert_fusion.2
  134.7 2.0 convolution_convert_fusion.1
  136.8 0.2 copy.61
  137.0 0.9 convolution_convert_fusion
  137.9 2.5 %copy.63 = bf16[16,128,512]{2,1,0:T(8,128)(2,1)} copy(bf16[16,128,512]{2,0,1:T(8,128)(2,1)S(1)} %convolution_convert_fusion) | data formatting | bytes 4194304 | tf_op jit(solution)/shard_map/convert_element_type | solution.py:393
  140.4 6.0 %all-to-all-start.4 = ((bf16[16,128,512]{2,1,0:T(8,128)(2,1)}), bf16[16,128,512]{2,1,0:T(8,128)(2,1)}, u32[]{:S(2)}, u32[]{:S(2)}) async-start(bf16[16,128,512]{2,1,0:T(8,128)(2,1)} %copy.63), calls=%async_computation.4 | async-start | bytes 4194304 | tf_op jit(solution)/shard_map/all_to_all | solution.py:394
  146.4 0.1 copy.55
  146.6 0.1 lt.62
  146.6 0.1 copy.57
  146.7 0.1 eq.47
  146.8 0.1 fusion.15
  146.9 0.1 reduce_window_sum.11
  147.0 0.2 select_reduce_fusion
  147.2 0.1 reduce_sum.39
  147.3 0.1 copy.56
  147.4 0.1 convert_reduce_fusion.1
  147.5 47.5 %all-to-all-done.4 = bf16[16,128,512]{2,1,0:T(8,128)(2,1)} async-done(((bf16[16,128,512]{2,1,0:T(8,128)(2,1)}), bf16[16,128,512]{2,1,0:T(8,128)(2,1)}, u32[]{:S(2)}, u32[]{:S(2)}) %all-to-all-start.4) | async-done | bytes 2097184 | tf_op jit(solution)/shard_map/all_to_all | solution.py:394
  194.9 2.9 %fusion.2 = bf16[4,128,512]{2,0,1:T(4,128)(2,1)S(1)} fusion(bf16[16,128,512]{2,1,0:T(8,128)(2,1)} %all-to-all-done.4, bf16[4,16]{1,0:T(4,128)(2,1)S(1)} %convert_reduce_fusion.1), kind=kOutput, calls=%fused_computation.5 | convolution fusion | flops 8388608 | bytes 2621568 | tf_op jit(solution)/shard_map/rg,gtc->rtc/dot_general | solution.py:396
  197.8 0.1 copy.75.pair_ref
  197.9 5.8 %decoder.1 = bf16[4,256,778]{2,1,0:T(8,128)(2,1)S(1)} custom-call(bf16[4,128,512]{2,1,0:T(8,128)(2,1)S(1)} %copy.75.pair_ref, bf16[778,256]{1,0:T(8,128)(2,1)S(1)} %copy-done.12), custom_call_target="tpu_custom_call" | custom-call | tf_op jit(solution)/shard_map/decoder/pallas_call | solution.py:443
  203.7 1.3 copy-done.5
  205.0 4.0 %copy.67 = bf16[4,256,778]{1,0,2:T(4,128)(2,1)} copy(bf16[4,256,778]{2,1,0:T(8,128)(2,1)} %copy-done.5) | data formatting | bytes 3186688
  (52 shorter events, 0.5 us)
Async XLA Ops:
  0.6 14.2 %copy-start = (bf16[1,1024,1280]{2,1,0:T(8,128)(2,1)S(1)}, bf16[1,1024,1280]{2,1,0:T(8,128)(2,1)}, u32[]{:S(2)}) copy-start(bf16[1,1024,1280]{2,1,0:T(8,128)(2,1)} %param.12) | copy-start | bytes 7864324
  3.2 11.5 %copy-start.1 = (bf16[1024,640]{1,0:T(8,128)(2,1)}, bf16[1024,640]{1,0:T(8,128)(2,1)S(1)}, u32[]{:S(2)}) copy-start(bf16[1024,640]{1,0:T(8,128)(2,1)S(1)} %get-tuple-element.28.v_ref) | copy-start | bytes 3932164
  3.3 11.5 %copy-start.3 = (bf16[1024,640]{1,0:T(8,128)(2,1)}, bf16[1024,640]{1,0:T(8,128)(2,1)S(1)}, u32[]{:S(2)}) copy-start(bf16[1024,640]{1,0:T(8,128)(2,1)S(1)} %get-tuple-element.30.k_ref) | copy-start | bytes 3932164
  3.3 2.6 %copy-start.6 = (bf16[640,1280]{1,0:T(8,128)(2,1)S(1)}, bf16[640,1280]{1,0:T(8,128)(2,1)}, u32[]{:S(2)}) copy-start(bf16[640,1280]{1,0:T(8,128)(2,1)} %w_ref.6) | copy-start | bytes 4915204
  14.8 2.4 %collective-permute-start = (bf16[512,640]{1,0:T(8,128)(2,1)}, bf16[512,640]{1,0:T(8,128)(2,1)}, u32[]{:S(2)}, u32[]{:S(2)}) collective-permute-start(bf16[512,640]{1,0:T(8,128)(2,1)} %get-tuple-element.11), channel_id=1, source_target_pairs={{0,1},{1,0},{2,3},{3,2},{4,5},{5,4},{6,7},{7,6},{8,9},{9,8},{10,11... | collective-permute-start | bytes 1966088 | tf_op jit(solution)/shard_map/ppermute | solution.py:293
  19.4 23.8 %all-to-all-start = ((bf16[16,32,640]{2,1,0:T(8,128)(2,1)}), bf16[16,32,640]{2,1,0:T(8,128)(2,1)S(1)}, u32[]{:S(2)}, u32[]{:S(2)}) async-start(bf16[16,32,640]{2,1,0:T(8,128)(2,1)} %bitcast.51), calls=%async_computation | async-start | bytes 1310720 | tf_op jit(solution)/shard_map/all_to_all | solution.py:335
  26.5 1.3 copy-start.2
  27.8 1.3 copy-start.4
  29.2 1.4 copy-start.7
  30.6 1.1 copy-start.10
  31.7 10.3 %copy-start.13 = (bf16[16,1,32,640]{3,2,1,0:T(8,128)(2,1)S(1)}, bf16[16,1,32,640]{3,2,1,0:T(8,128)(2,1)}, u32[]{:S(2)}) copy-start(bf16[16,1,32,640]{3,2,1,0:T(8,128)(2,1)} %get-tuple-element.32) | copy-start | bytes 1966084
  39.9 2.2 %collective-permute-start.3 = (bf16[512,640]{1,0:T(8,128)(2,1)S(1)}, bf16[512,640]{1,0:T(8,128)(2,1)S(1)}, u32[]{:S(2)}, u32[]{:S(2)}) collective-permute-start(bf16[512,640]{1,0:T(8,128)(2,1)S(1)} %get-tuple-element.15), channel_id=1, source_target_pairs={{0,1},{1,0},{2,3},{3,2},{4,5},{5,4},{6,7},{7,6},{8,9},{9,8},{10,11... | collective-permute-start | bytes 1966088 | tf_op jit(solution)/shard_map/ppermute | solution.py:293
  42.0 8.2 %copy-start.16 = (bf16[1280]{0:T(1024)(128)(2,1)S(1)}, bf16[1280]{0:T(1024)(128)(2,1)}, u32[]{:S(2)}) copy-start(bf16[1280]{0:T(1024)(128)(2,1)} %param.15) | copy-start | bytes 7684
  43.2 7.1 %collective-permute-start.1 = (bf16[16,32,640]{2,1,0:T(8,128)(2,1)S(1)}, bf16[16,32,640]{2,1,0:T(8,128)(2,1)}, u32[]{:S(2)}, u32[]{:S(2)}) collective-permute-start(bf16[16,32,640]{2,1,0:T(8,128)(2,1)S(1)} %all-to-all-done.mid_mine), channel_id=1, source_target_pairs={{0,1},{1,0},{2,3},{3,2},{4,5},{5,4},{6,7},{7,6},{8,9},{9,8},{10,11... | collective-permute-start | bytes 1966088 | tf_op jit(solution)/shard_map/ppermute | solution.py:293
  43.3 23.4 %all-to-all-start.2 = ((bf16[16,32,640]{2,1,0:T(8,128)(2,1)}), bf16[16,32,640]{2,1,0:T(8,128)(2,1)}, u32[]{:S(2)}, u32[]{:S(2)}) async-start(bf16[16,32,640]{2,1,0:T(8,128)(2,1)} %bitcast.52), calls=%async_computation.2 | async-start | bytes 1310720 | tf_op jit(solution)/shard_map/all_to_all | solution.py:335
  50.3 1.4 copy-start.8
  65.9 0.8 copy-start.11
  66.7 2.4 %collective-permute-start.2 = (bf16[16,32,640]{2,1,0:T(8,128)(2,1)}, bf16[16,32,640]{2,1,0:T(8,128)(2,1)}, u32[]{:S(2)}, u32[]{:S(2)}) collective-permute-start(bf16[16,32,640]{2,1,0:T(8,128)(2,1)} %get-tuple-element.13), channel_id=1, source_target_pairs={{0,1},{1,0},{2,3},{3,2},{4,5},{5,4},{6,7},{7,6},{8,9},{9,8},{10,11... | collective-permute-start | bytes 1966088 | tf_op jit(solution)/shard_map/ppermute | solution.py:293
  66.7 11.7 %collective-permute-start.4 = (bf16[16,32,640]{2,1,0:T(8,128)(2,1)}, bf16[16,32,640]{2,1,0:T(8,128)(2,1)}, u32[]{:S(2)}, u32[]{:S(2)}) collective-permute-start(bf16[16,32,640]{2,1,0:T(8,128)(2,1)} %all-to-all-done.2.mid_mine), channel_id=1, source_target_pairs={{0,1},{1,0},{2,3},{3,2},{4,5},{5,4},{6,7},{7,6},{8,9},{9,8},{10,11... | collective-permute-start | bytes 1966088 | tf_op jit(solution)/shard_map/ppermute | solution.py:293
  71.5 26.3 %all-to-all-start.1 = ((bf16[16,32,640]{2,1,0:T(8,128)(2,1)}), bf16[16,32,640]{2,1,0:T(8,128)(2,1)S(1)}, u32[]{:S(2)}, u32[]{:S(2)}) async-start(bf16[16,32,640]{2,1,0:T(8,128)(2,1)} %add_convert_fusion.1), calls=%async_computation.1 | async-start | bytes 1310720 | tf_op jit(solution)/shard_map/all_to_all | solution.py:350
  78.4 1.4 copy-start.9
  93.5 2.2 %collective-permute-start.5 = (bf16[16,32,640]{2,1,0:T(8,128)(2,1)S(1)}, bf16[16,32,640]{2,1,0:T(8,128)(2,1)S(1)}, u32[]{:S(2)}, u32[]{:S(2)}) collective-permute-start(bf16[16,32,640]{2,1,0:T(8,128)(2,1)S(1)} %get-tuple-element.17), channel_id=1, source_target_pairs={{0,1},{1,0},{2,3},{3,2},{4,5},{5,4},{6,7},{7,6},{8,9},{9,8},{10,11... | collective-permute-start | bytes 1966088 | tf_op jit(solution)/shard_map/ppermute | solution.py:293
  95.6 9.1 %copy-start.14 = (s32[16,3]{0,1:T(4,128)S(1)}, s32[16,3]{0,1:T(4,128)}, u32[]{:S(2)}) copy-start(s32[16,3]{0,1:T(4,128)} %param.23) | copy-start | bytes 580
  95.6 9.1 %copy-start.17 = (s32[16,3]{0,1:T(4,128)S(1)}, s32[16,3]{0,1:T(4,128)}, u32[]{:S(2)}) copy-start(s32[16,3]{0,1:T(4,128)} %param.22) | copy-start | bytes 580
  97.8 23.2 %all-to-all-start.3 = ((bf16[16,32,640]{2,1,0:T(8,128)(2,1)}), bf16[16,32,640]{2,1,0:T(8,128)(2,1)}, u32[]{:S(2)}, u32[]{:S(2)}) async-start(bf16[16,32,640]{2,1,0:T(8,128)(2,1)} %add_convert_fusion), calls=%async_computation.3 | async-start | bytes 1310720 | tf_op jit(solution)/shard_map/all_to_all | solution.py:350
  122.2 5.2 %copy-start.15 = (bf16[1280]{0:T(1024)(128)(2,1)S(1)}, bf16[1280]{0:T(1024)(128)(2,1)}, u32[]{:S(2)}) copy-start(bf16[1280]{0:T(1024)(128)(2,1)} %param.18) | copy-start | bytes 7684
  122.2 5.3 %copy-start.18 = (s32[16]{0:T(128)S(1)}, s32[16]{0:T(128)}, u32[]{:S(2)}) copy-start(s32[16]{0:T(128)} %param.21) | copy-start | bytes 196
  127.4 2.1 collective-permute-start.6
  127.5 5.2 %copy-start.19 = (bf16[2,1280,256]{2,1,0:T(8,128)(2,1)S(1)}, bf16[2,1280,256]{2,1,0:T(8,128)(2,1)}, u32[]{:S(2)}) copy-start(bf16[2,1280,256]{2,1,0:T(8,128)(2,1)} %param.19) | copy-start | bytes 3932164
  140.4 54.6 %all-to-all-start.4 = ((bf16[16,128,512]{2,1,0:T(8,128)(2,1)}), bf16[16,128,512]{2,1,0:T(8,128)(2,1)}, u32[]{:S(2)}, u32[]{:S(2)}) async-start(bf16[16,128,512]{2,1,0:T(8,128)(2,1)} %copy.63), calls=%async_computation.4 | async-start | bytes 4194304 | tf_op jit(solution)/shard_map/all_to_all | solution.py:394
  146.4 51.5 %copy-start.12 = (bf16[778,256]{1,0:T(8,128)(2,1)S(1)}, bf16[778,256]{1,0:T(8,128)(2,1)}, u32[]{:S(2)}) copy-start(bf16[778,256]{1,0:T(8,128)(2,1)} %query_ref.1) | copy-start | bytes 1195012
  203.7 1.3 copy-start.5

commit v3 on v2

--- a/solution.py
+++ b/solution.py
@@ -127,7 +127,7 @@
         MAXC * TILE, model_width
     )
     return decode(
-        crop_norm, decoder_kv_w, vertex_queries, crop_counts, crop_owner
+        [crop_norm], decoder_kv_w, vertex_queries, crop_counts, crop_owner
     ), stream_part
 
 
@@ -352,33 +352,30 @@
     stream_part = jnp.stack(returned, axis=1).reshape(1, patches, half)
     frame_id = lax.axis_index("frame")
     my_tiles = lax.dynamic_index_in_dim(crop_tiles, frame_id, 0, keepdims=False)
-    tile_view = stream_part.reshape(patches // TILE, TILE, half)
-    crop_mine = jnp.take(tile_view, my_tiles, axis=0).reshape(MAXC * TILE, half)
-    crop_other = swap(crop_mine)
-    crop_rows = jnp.where(
-        here == 0,
-        jnp.concatenate([crop_mine, crop_other], axis=1),
-        jnp.concatenate([crop_other, crop_mine], axis=1),
-    )
-    crop_norm = layer_norm(crop_rows.astype(jnp.float32), decoder_gain)
-    return decode(
-        crop_norm, decoder_kv_w, vertex_queries, crop_counts, crop_owner
-    ), stream_part
-
-
-def decode(crop_norm, decoder_kv_w, vertex_queries, crop_counts, crop_owner):
+    norms = []
+    for part in returned:
+        tile_view = part.reshape(patches // TILE, TILE // CHUNKS, half)
+        crop_mine = jnp.concatenate(
+            [
+                lax.dynamic_index_in_dim(tile_view, my_tiles[slot], 0, keepdims=False)
+                for slot in range(MAXC)
+            ],
+            axis=0,
+        )
+        crop_other = swap(crop_mine)
+        crop_rows = jnp.where(
+            here == 0,
+            jnp.concatenate([crop_mine, crop_other], axis=1),
+            jnp.concatenate([crop_other, crop_mine], axis=1),
+        )
+        norms.append(layer_norm(crop_rows.astype(jnp.float32), decoder_gain))
+    return decode(norms, decoder_kv_w, vertex_queries, crop_counts, crop_owner), stream_part
+
+
+def decode(crop_norms, decoder_kv_w, vertex_queries, crop_counts, crop_owner):
     frame_id = lax.axis_index("frame")
     frames_all = crop_owner.shape[0]
     dec_local = decoder_kv_w.shape[2]
-    crop_keys = jnp.dot(crop_norm, decoder_kv_w[0], preferred_element_type=jnp.float32).astype(
-        jnp.bfloat16
-    )
-    crop_values = jnp.dot(crop_norm, decoder_kv_w[1], preferred_element_type=jnp.float32).astype(
-        jnp.bfloat16
-    )
-    crop_pairs = jnp.concatenate([crop_keys, crop_values], axis=1).reshape(
-        MAXC, TILE, 2 * dec_local
-    )
     live_slots, slot_index = crop_slots(crop_counts, crop_owner)
     targets = frame_id * RCAP + jnp.arange(RCAP, dtype=jnp.int32)
     choose = ((slot_index[None, :] == targets[:, None]) & live_slots[None, :]).astype(jnp.float32)
@@ -388,14 +385,27 @@
     to_owner = (
         (my_owner[None, :] == jnp.arange(frames_all, dtype=jnp.int32)[:, None]) & my_live[None, :]
     ).astype(jnp.bfloat16)
-    outgoing = jnp.einsum(
-        "nm,mtc->ntc", to_owner, crop_pairs, preferred_element_type=jnp.float32
-    ).astype(jnp.bfloat16)
-    incoming = lax.all_to_all(outgoing, "frame", split_axis=0, concat_axis=0, tiled=True)
     by_frame = choose.reshape(RCAP, frames_all, MAXC).sum(axis=2).astype(jnp.bfloat16)
-    slot_pairs = jnp.einsum(
-        "rg,gtc->rtc", by_frame, incoming, preferred_element_type=jnp.float32
-    ).astype(jnp.bfloat16)
+    pieces = []
+    for crop_norm in crop_norms:
+        crop_keys = jnp.dot(crop_norm, decoder_kv_w[0], preferred_element_type=jnp.float32).astype(
+            jnp.bfloat16
+        )
+        crop_values = jnp.dot(crop_norm, decoder_kv_w[1], preferred_element_type=jnp.float32).astype(
+            jnp.bfloat16
+        )
+        crop_pairs = jnp.concatenate([crop_keys, crop_values], axis=1).reshape(
+            MAXC, -1, 2 * dec_local
+        )
+        outgoing = jnp.einsum(
+            "nm,mtc->ntc", to_owner, crop_pairs, preferred_element_type=jnp.float32
+        ).astype(jnp.bfloat16)
+        incoming = lax.all_to_all(outgoing, "frame", split_axis=0, concat_axis=0, tiled=True)
+        piece = jnp.einsum(
+            "rg,gtc->rtc", by_frame, incoming, preferred_element_type=jnp.float32
+        ).astype(jnp.bfloat16)
+        pieces.append(piece)
+    slot_pairs = jnp.concatenate(pieces, axis=1)
     if dec_local % 128 == 0:
         return vertex_decoder(slot_pairs, vertex_queries)
     heads_dec = dec_local // DEC_HD

time: 210 us -> 201 us (0.957)
  waiting for transfers between devices: 71.5 us -> 52.2 us
  starting transfers between devices: 34.8 us -> 40.7 us
  between operations: 0.99 us -> 6.72 us
    all_to_all x1 -> x2, waiting for transfers between devices: 47.5 us -> 36.3 us  [decode(): lax.all_to_all(outgoing, 'frame', split_axis=0, concat_axis=0, tiled=True)]
    all_to_all x2, waiting for transfers between devices: 15.9 us -> 6.96 us  [on_device_pair(): lax.all_to_all(final_mine, 'frame', split_axis=0, concat_axis=0, tiled=True)]
    all_to_all x1 -> x2, starting transfers between devices: 6.01 us -> 11.8 us  [decode(): lax.all_to_all(outgoing, 'frame', split_axis=0, concat_axis=0, tiled=True)]
    gather x1 -> x0, local copies, waits for them, and re-layouts: 2.71 us -> none  [on_device_pair(): crop_mine = jnp.take(tile_view, my_tiles, axis=0).reshape(MAXC * TILE, half)]
    ppermute x7 -> x8, waiting for transfers between devices: 8.11 us -> 8.93 us  [swap(): return lax.ppermute(values, 'mp', [(0, 1), (1, 0)])]
    unnamed x42 -> x50, local copies, waits for them, and re-layouts: 15.8 us -> 16.5 us
  transfers between devices with their start and end apart: 12 -> 14, of which waited for: 7 -> 8; matrix products, arithmetic and copies ran while one was open for 4% -> 10% of each run, Pallas kernels for 17% -> 18%
where the time goes in v3:
time: 201 us; the launch traced here: 199 us
  waiting for transfers between devices  52.2 us (26%)
  Pallas kernels  50.6 us (25%)
  starting transfers between devices  40.7 us (20%)
  local copies, waits for them, and re-layouts  28.6 us (14%)
  other arithmetic  13.4 us (7%)
  between operations  6.72 us (3%)
  matrix products  6.4 us (3%)
    all_to_all x2, waiting for transfers between devices, decode(): lax.all_to_all(outgoing, 'frame', split_axis=0, concat_axis=0, tiled=True)  36.3 us
    pallas_call x2, Pallas kernels, temporal_attention(): pl.pallas_call(temporal_kernel, grid=(patch_rows // PATCHES,), in_specs=[...  27.8 us
    pallas_call x2, Pallas kernels, spatial_attention(): pl.pallas_call(spatial_kernel, grid=(patches // ROWS,), in_specs=[pl.Bloc...  17.1 us
    unnamed x50, local copies, waits for them, and re-layouts  16.5 us
    all_to_all x2, starting transfers between devices, on_device_pair(): lax.all_to_all(middle.reshape(frames_all, part_rows, half), 'frame', spli...  14.1 us
    all_to_all x2, starting transfers between devices, on_device_pair(): lax.all_to_all(final_mine, 'frame', split_axis=0, concat_axis=0, tiled=True)  14 us
    all_to_all x2, starting transfers between devices, decode(): lax.all_to_all(outgoing, 'frame', split_axis=0, concat_axis=0, tiled=True)  11.8 us
    ppermute x8, waiting for transfers between devices, swap(): return lax.ppermute(values, 'mp', [(0, 1), (1, 0)])  8.93 us
  transfers between devices with their start and end apart: 14, of which 8 were waited for; matrix products, arithmetic and copies ran while one was open for 10% of the time, Pallas kernels for 18%

profile of v3, /device:TPU:14, one launch (start us, length us, event | category | flops | bytes accessed | tf_op | source)
XLA Modules:
  0.0 198.7 jit_solution(1515610799821548499)
XLA Ops:
  0.6 2.6 %slice_bitcast_fusion = (bf16[1024,640]{1,0:T(8,128)(2,1)S(1)}, bf16[1,1024,1,640]{3,1,2,0:T(8,128)(2,1)S(1)}, bf16[1024,640]{1,0:T(8,128)(2,1)S(1)}) fusion(bf16[1,1024,3,640]{3,1,2,0:T(8,128)(2,1)} %param.13), kind=kLoop, calls=%fused_computation.9 | loop fusion | bytes 7864320 | tf_op jit(solution)/shard_map/squeeze | solution.py:326
  3.3 1.0 fusion.42
  4.2 0.3 copy-done.1
  4.5 0.4 copy-done.3
  4.9 0.9 copy-done.6
  5.9 8.9 %spatial.2 = (bf16[512,640]{1,0:T(8,128)(2,1)S(1)}, bf16[512,640]{1,0:T(8,128)(2,1)}) custom-call(bf16[512,640]{1,0:T(8,128)(2,1)S(1)} %bitcast.63, bf16[1024,640]{1,0:T(8,128)(2,1)S(1)} %get-tuple-element.34.k_ref, bf16[1024,640]{1,0:T(8,128)(2,1)S(1)} %get-tuple-element.32.v_ref, bf16[640,1280]{1,0:T(8,128)(2,1)S(1)} %copy-done.6), custom_call_target="tpu_custom_call" | custom-call | tf_op jit(solution)/shard_map/spatial/pallas_call | solution.py:199
  14.9 1.0 fusion.41
  15.9 1.3 collective-permute-done
  17.2 2.2 %fusion.1 = bf16[512,640]{1,0:T(8,128)(2,1)} fusion(bf16[512,640]{1,0:T(8,128)(2,1)} %collective-permute-done, bf16[512,640]{1,0:T(8,128)(2,1)S(1)} %get-tuple-element.10, bf16[16,1,32,640]{3,2,1,0:T(8,128)(2,1)S(1)} %get-tuple-element.35), kind=kLoop, calls=%fused_computation.6 | loop fusion | flops 1966080 | bytes 2621440 | tf_op jit(solution)/shard_map/convert_element_type | solution.py:298
  19.4 7.1 %all-to-all-start = ((bf16[16,32,640]{2,1,0:T(8,128)(2,1)}), bf16[16,32,640]{2,1,0:T(8,128)(2,1)S(1)}, u32[]{:S(2)}, u32[]{:S(2)}) async-start(bf16[16,32,640]{2,1,0:T(8,128)(2,1)} %bitcast.68), calls=%async_computation | async-start | bytes 1310720 | tf_op jit(solution)/shard_map/all_to_all | solution.py:335
  26.5 1.3 copy-done.2
  27.9 1.3 copy-done.4
  29.2 1.4 copy-done.7
  30.6 1.1 copy-done.10
  31.7 8.2 %spatial.3 = (bf16[512,640]{1,0:T(8,128)(2,1)S(1)}, bf16[512,640]{1,0:T(8,128)(2,1)S(1)}) custom-call(bf16[512,640]{1,0:T(8,128)(2,1)S(1)} %bitcast.62, bf16[1024,640]{1,0:T(8,128)(2,1)S(1)} %copy-done.4, bf16[1024,640]{1,0:T(8,128)(2,1)S(1)} %copy-done.2, bf16[640,1280]{1,0:T(8,128)(2,1)S(1)} %copy-done.7), custom_call_target="tpu_custom_call" | custom-call | tf_op jit(solution)/shard_map/spatial/pallas_call | solution.py:199
  40.0 2.1 %collective-permute-done.4 = bf16[512,640]{1,0:T(8,128)(2,1)S(1)} collective-permute-done((bf16[512,640]{1,0:T(8,128)(2,1)S(1)}, bf16[512,640]{1,0:T(8,128)(2,1)S(1)}, u32[]{:S(2)}, u32[]{:S(2)}) %collective-permute-start.4) | collective-permute-done | bytes 655392 | tf_op jit(solution)/shard_map/ppermute | solution.py:293
  42.0 1.1 fusion
  43.2 0.1 collective-permute-start.1
  43.3 6.9 %all-to-all-start.3 = ((bf16[16,32,640]{2,1,0:T(8,128)(2,1)}), bf16[16,32,640]{2,1,0:T(8,128)(2,1)}, u32[]{:S(2)}, u32[]{:S(2)}) async-start(bf16[16,32,640]{2,1,0:T(8,128)(2,1)} %bitcast.69), calls=%async_computation.3 | async-start | bytes 1310720 | tf_op jit(solution)/shard_map/all_to_all | solution.py:335
  50.3 1.4 copy-done.8
  51.7 14.2 %temporal.2 = (bf16[16,32,640]{2,1,0:T(8,128)(2,1)S(1)}, bf16[16,32,640]{2,1,0:T(8,128)(2,1)}) custom-call(bf16[16,32,640]{2,1,0:T(8,128)(2,1)S(1)} %all-to-all-done.mid_mine, bf16[16,32,640]{2,1,0:T(8,128)(2,1)} %collective-permute-done.1.mid_other, bf16[1,1280]{1,0:T(2,128)(2,1)S(1)} %reshape.132.gain_ref, bf16[3,1280,640]{2,1,0:T(8,128)(2,1)} %w_ref.7, ...), custom_call_target="tpu_custom_call" | custom-call | tf_op jit(solution)/shard_map/temporal/pallas_call | solution.py:271
  65.9 0.8 copy-done.11
  66.7 0.5 collective-permute-start.5
  67.3 1.9 collective-permute-done.2
  69.2 2.4 %add_convert_fusion.1 = bf16[16,32,640]{2,1,0:T(8,128)(2,1)} fusion(bf16[16,32,640]{2,1,0:T(8,128)(2,1)} %collective-permute-done.2, bf16[16,32,640]{2,1,0:T(8,128)(2,1)} %copy-done.11, bf16[16,32,640]{2,1,0:T(8,128)(2,1)S(1)} %all-to-all-done.mid_mine), kind=kLoop, calls=%fused_computation.8 | loop fusion | flops 1966080 | bytes 2621440 | tf_op jit(solution)/shard_map/convert_element_type | solution.py:298
  71.5 6.9 %all-to-all-start.1 = ((bf16[16,32,640]{2,1,0:T(8,128)(2,1)}), bf16[16,32,640]{2,1,0:T(8,128)(2,1)S(1)}, u32[]{:S(2)}, u32[]{:S(2)}) async-start(bf16[16,32,640]{2,1,0:T(8,128)(2,1)} %add_convert_fusion.1), calls=%async_computation.1 | async-start | bytes 1310720 | tf_op jit(solution)/shard_map/all_to_all | solution.py:350
  78.5 1.4 copy-done.9
  79.9 13.6 %temporal.3 = (bf16[16,32,640]{2,1,0:T(8,128)(2,1)S(1)}, bf16[16,32,640]{2,1,0:T(8,128)(2,1)S(1)}) custom-call(bf16[16,32,640]{2,1,0:T(8,128)(2,1)} %all-to-all-done.3.mid_mine, bf16[16,32,640]{2,1,0:T(8,128)(2,1)} %collective-permute-done.5.mid_other, bf16[1,1280]{1,0:T(2,128)(2,1)S(1)} %reshape.132.gain_ref, bf16[3,1280,640]{2,1,0:T(8,128)(2,1)} %w_ref.7, ...), custom_call_target="tpu_custom_call" | custom-call | tf_op jit(solution)/shard_map/temporal/pallas_call | solution.py:271
  93.6 2.1 %collective-permute-done.6 = bf16[16,32,640]{2,1,0:T(8,128)(2,1)S(1)} collective-permute-done((bf16[16,32,640]{2,1,0:T(8,128)(2,1)S(1)}, bf16[16,32,640]{2,1,0:T(8,128)(2,1)S(1)}, u32[]{:S(2)}, u32[]{:S(2)}) %collective-permute-start.6) | collective-permute-done | bytes 655392 | tf_op jit(solution)/shard_map/ppermute | solution.py:293
  95.7 2.2 %add_convert_fusion = bf16[16,32,640]{2,1,0:T(8,128)(2,1)} fusion(bf16[16,32,640]{2,1,0:T(8,128)(2,1)S(1)} %collective-permute-done.6, bf16[16,32,640]{2,1,0:T(8,128)(2,1)S(1)} %get-tuple-element.16, bf16[16,32,640]{2,1,0:T(8,128)(2,1)} %all-to-all-done.3.mid_mine), kind=kLoop, calls=%fused_computation.7 | loop fusion | flops 1966080 | bytes 2621440 | tf_op jit(solution)/shard_map/convert_element_type | solution.py:298
  97.9 7.1 %all-to-all-start.4 = ((bf16[16,32,640]{2,1,0:T(8,128)(2,1)}), bf16[16,32,640]{2,1,0:T(8,128)(2,1)}, u32[]{:S(2)}, u32[]{:S(2)}) async-start(bf16[16,32,640]{2,1,0:T(8,128)(2,1)} %add_convert_fusion), calls=%async_computation.4 | async-start | bytes 1310720 | tf_op jit(solution)/shard_map/all_to_all | solution.py:350
  104.9 0.2 constant_dynamic-slice_fusion
  105.1 0.6 fusion.43
  111.5 0.6 copy-done.14
  112.1 0.7 pad_maximum_fusion.2
  112.8 0.7 dynamic_slice.34
  113.5 0.7 iota_compare_fusion.3
  114.2 7.0 %all-to-all-done.4 = bf16[16,32,640]{2,1,0:T(8,128)(2,1)} async-done(((bf16[16,32,640]{2,1,0:T(8,128)(2,1)}), bf16[16,32,640]{2,1,0:T(8,128)(2,1)}, u32[]{:S(2)}, u32[]{:S(2)}) %all-to-all-start.4) | async-done | bytes 655392 | tf_op jit(solution)/shard_map/all_to_all | solution.py:350
  121.2 1.1 dynamic-slice_bitcast_fusion.2
  122.3 1.5 convert_reduce_fusion.1
  123.8 0.3 fusion.13
  124.1 0.4 convolution_convert_fusion.5
  124.5 0.4 convolution_convert_fusion.4
  124.8 0.6 convolution_convert_fusion.1
  125.5 1.5 copy.64
  127.0 6.0 %all-to-all-start.2 = ((bf16[16,64,512]{2,1,0:T(8,128)(2,1)}), bf16[16,64,512]{2,1,0:T(8,128)(2,1)}, u32[]{:S(2)}, u32[]{:S(2)}) async-start(bf16[16,64,512]{2,1,0:T(8,128)(2,1)} %copy.64), calls=%async_computation.2 | async-start | bytes 2097152 | tf_op jit(solution)/shard_map/all_to_all | solution.py:403
  133.1 1.5 collective-permute-done.7
  134.6 0.2 convert_reduce_fusion
  134.8 0.3 fusion.10
  135.1 0.4 convolution_convert_fusion.3
  135.5 0.4 convolution_convert_fusion.2
  135.9 0.6 convolution_convert_fusion
  136.5 1.5 copy.69
  138.0 18.6 %all-to-all-done.2 = bf16[16,64,512]{2,1,0:T(8,128)(2,1)} async-done(((bf16[16,64,512]{2,1,0:T(8,128)(2,1)}), bf16[16,64,512]{2,1,0:T(8,128)(2,1)}, u32[]{:S(2)}, u32[]{:S(2)}) %all-to-all-start.2) | async-done | bytes 1048608 | tf_op jit(solution)/shard_map/all_to_all | solution.py:403
  156.6 5.8 %all-to-all-start.5 = ((bf16[16,64,512]{2,1,0:T(8,128)(2,1)}), bf16[16,64,512]{2,1,0:T(8,128)(2,1)}, u32[]{:S(2)}, u32[]{:S(2)}) async-start(bf16[16,64,512]{2,1,0:T(8,128)(2,1)} %copy.69), calls=%async_computation.5 | async-start | bytes 2097152 | tf_op jit(solution)/shard_map/all_to_all | solution.py:403
  163.1 0.2 select_reduce_fusion
  163.5 1.2 pad_maximum_fusion
  164.8 1.2 copy.72
  166.0 1.9 fusion.8
  168.0 17.7 %all-to-all-done.5 = bf16[16,64,512]{2,1,0:T(8,128)(2,1)} async-done(((bf16[16,64,512]{2,1,0:T(8,128)(2,1)}), bf16[16,64,512]{2,1,0:T(8,128)(2,1)}, u32[]{:S(2)}, u32[]{:S(2)}) %all-to-all-start.5) | async-done | bytes 1048608 | tf_op jit(solution)/shard_map/all_to_all | solution.py:403
  185.7 1.9 fusion.6
  187.7 5.8 %decoder.1 = bf16[4,256,778]{2,1,0:T(8,128)(2,1)S(1)} custom-call(bf16[4,128,512]{2,1,0:T(8,128)(2,1)S(1)} %pad_maximum_fusion.1.pair_ref, bf16[778,256]{1,0:T(8,128)(2,1)S(1)} %copy-done.12), custom_call_target="tpu_custom_call" | custom-call | tf_op jit(solution)/shard_map/decoder/pallas_call | solution.py:453
  193.5 1.3 copy-done.5
  194.7 4.0 %copy.73 = bf16[4,256,778]{1,0,2:T(4,128)(2,1)} copy(bf16[4,256,778]{2,1,0:T(8,128)(2,1)} %copy-done.5) | data formatting | bytes 3186688
  (74 shorter events, 1.5 us)
Async XLA Ops:
  0.6 14.2 %copy-start = (bf16[1,1024,1280]{2,1,0:T(8,128)(2,1)S(1)}, bf16[1,1024,1280]{2,1,0:T(8,128)(2,1)}, u32[]{:S(2)}) copy-start(bf16[1,1024,1280]{2,1,0:T(8,128)(2,1)} %param.12) | copy-start | bytes 7864324
  3.2 1.3 copy-start.1
  3.3 1.7 copy-start.3
  3.3 2.6 %copy-start.6 = (bf16[640,1280]{1,0:T(8,128)(2,1)S(1)}, bf16[640,1280]{1,0:T(8,128)(2,1)}, u32[]{:S(2)}) copy-start(bf16[640,1280]{1,0:T(8,128)(2,1)} %w_ref.6) | copy-start | bytes 4915204
  14.8 2.4 %collective-permute-start = (bf16[512,640]{1,0:T(8,128)(2,1)}, bf16[512,640]{1,0:T(8,128)(2,1)}, u32[]{:S(2)}, u32[]{:S(2)}) collective-permute-start(bf16[512,640]{1,0:T(8,128)(2,1)} %get-tuple-element.11), channel_id=1, source_target_pairs={{0,1},{1,0},{2,3},{3,2},{4,5},{5,4},{6,7},{7,6},{8,9},{9,8},{10,11... | collective-permute-start | bytes 1966088 | tf_op jit(solution)/shard_map/ppermute | solution.py:293
  19.4 23.8 %all-to-all-start = ((bf16[16,32,640]{2,1,0:T(8,128)(2,1)}), bf16[16,32,640]{2,1,0:T(8,128)(2,1)S(1)}, u32[]{:S(2)}, u32[]{:S(2)}) async-start(bf16[16,32,640]{2,1,0:T(8,128)(2,1)} %bitcast.68), calls=%async_computation | async-start | bytes 1310720 | tf_op jit(solution)/shard_map/all_to_all | solution.py:335
  26.5 1.3 copy-start.2
  27.9 1.3 copy-start.4
  29.2 1.4 copy-start.7
  30.6 1.1 copy-start.10
  31.7 10.3 %copy-start.13 = (bf16[16,1,32,640]{3,2,1,0:T(8,128)(2,1)S(1)}, bf16[16,1,32,640]{3,2,1,0:T(8,128)(2,1)}, u32[]{:S(2)}) copy-start(bf16[16,1,32,640]{3,2,1,0:T(8,128)(2,1)} %get-tuple-element.36) | copy-start | bytes 1966084
  39.9 2.2 %collective-permute-start.4 = (bf16[512,640]{1,0:T(8,128)(2,1)S(1)}, bf16[512,640]{1,0:T(8,128)(2,1)S(1)}, u32[]{:S(2)}, u32[]{:S(2)}) collective-permute-start(bf16[512,640]{1,0:T(8,128)(2,1)S(1)} %get-tuple-element.15), channel_id=1, source_target_pairs={{0,1},{1,0},{2,3},{3,2},{4,5},{5,4},{6,7},{7,6},{8,9},{9,8},{10,11... | collective-permute-start | bytes 1966088 | tf_op jit(solution)/shard_map/ppermute | solution.py:293
  43.2 7.1 %copy-start.19 = (bf16[1280]{0:T(1024)(128)(2,1)S(1)}, bf16[1280]{0:T(1024)(128)(2,1)}, u32[]{:S(2)}) copy-start(bf16[1280]{0:T(1024)(128)(2,1)} %param.15) | copy-start | bytes 7684
  43.2 7.1 %collective-permute-start.1 = (bf16[16,32,640]{2,1,0:T(8,128)(2,1)S(1)}, bf16[16,32,640]{2,1,0:T(8,128)(2,1)}, u32[]{:S(2)}, u32[]{:S(2)}) collective-permute-start(bf16[16,32,640]{2,1,0:T(8,128)(2,1)S(1)} %all-to-all-done.mid_mine), channel_id=1, source_target_pairs={{0,1},{1,0},{2,3},{3,2},{4,5},{5,4},{6,7},{7,6},{8,9},{9,8},{10,11... | collective-permute-start | bytes 1966088 | tf_op jit(solution)/shard_map/ppermute | solution.py:293
  43.3 23.4 %all-to-all-start.3 = ((bf16[16,32,640]{2,1,0:T(8,128)(2,1)}), bf16[16,32,640]{2,1,0:T(8,128)(2,1)}, u32[]{:S(2)}, u32[]{:S(2)}) async-start(bf16[16,32,640]{2,1,0:T(8,128)(2,1)} %bitcast.69), calls=%async_computation.3 | async-start | bytes 1310720 | tf_op jit(solution)/shard_map/all_to_all | solution.py:335
  50.3 1.4 copy-start.8
  65.9 0.8 copy-start.11
  66.7 2.4 %collective-permute-start.2 = (bf16[16,32,640]{2,1,0:T(8,128)(2,1)}, bf16[16,32,640]{2,1,0:T(8,128)(2,1)}, u32[]{:S(2)}, u32[]{:S(2)}) collective-permute-start(bf16[16,32,640]{2,1,0:T(8,128)(2,1)} %get-tuple-element.13), channel_id=1, source_target_pairs={{0,1},{1,0},{2,3},{3,2},{4,5},{5,4},{6,7},{7,6},{8,9},{9,8},{10,11... | collective-permute-start | bytes 1966088 | tf_op jit(solution)/shard_map/ppermute | solution.py:293
  66.7 11.7 %collective-permute-start.5 = (bf16[16,32,640]{2,1,0:T(8,128)(2,1)}, bf16[16,32,640]{2,1,0:T(8,128)(2,1)}, u32[]{:S(2)}, u32[]{:S(2)}) collective-permute-start(bf16[16,32,640]{2,1,0:T(8,128)(2,1)} %all-to-all-done.3.mid_mine), channel_id=1, source_target_pairs={{0,1},{1,0},{2,3},{3,2},{4,5},{5,4},{6,7},{7,6},{8,9},{9,8},{10,11... | collective-permute-start | bytes 1966088 | tf_op jit(solution)/shard_map/ppermute | solution.py:293
  71.5 26.3 %all-to-all-start.1 = ((bf16[16,32,640]{2,1,0:T(8,128)(2,1)}), bf16[16,32,640]{2,1,0:T(8,128)(2,1)S(1)}, u32[]{:S(2)}, u32[]{:S(2)}) async-start(bf16[16,32,640]{2,1,0:T(8,128)(2,1)} %add_convert_fusion.1), calls=%async_computation.1 | async-start | bytes 1310720 | tf_op jit(solution)/shard_map/all_to_all | solution.py:350
  78.5 1.4 copy-start.9
  93.5 2.2 %collective-permute-start.6 = (bf16[16,32,640]{2,1,0:T(8,128)(2,1)S(1)}, bf16[16,32,640]{2,1,0:T(8,128)(2,1)S(1)}, u32[]{:S(2)}, u32[]{:S(2)}) collective-permute-start(bf16[16,32,640]{2,1,0:T(8,128)(2,1)S(1)} %get-tuple-element.17), channel_id=1, source_target_pairs={{0,1},{1,0},{2,3},{3,2},{4,5},{5,4},{6,7},{7,6},{8,9},{9,8},{10,11... | collective-permute-start | bytes 1966088 | tf_op jit(solution)/shard_map/ppermute | solution.py:293
  97.8 7.1 %copy-start.17 = (s32[16,3]{0,1:T(4,128)S(1)}, s32[16,3]{0,1:T(4,128)}, u32[]{:S(2)}) copy-start(s32[16,3]{0,1:T(4,128)} %param.23) | copy-start | bytes 580
  97.8 7.1 %copy-start.20 = (s32[16,3]{0,1:T(4,128)S(1)}, s32[16,3]{0,1:T(4,128)}, u32[]{:S(2)}) copy-start(s32[16,3]{0,1:T(4,128)} %param.22) | copy-start | bytes 580
  97.8 15.0 %copy-start.18 = (bf16[1280]{0:T(1024)(128)(2,1)S(1)}, bf16[1280]{0:T(1024)(128)(2,1)}, u32[]{:S(2)}) copy-start(bf16[1280]{0:T(1024)(128)(2,1)} %param.18) | copy-start | bytes 7684
  97.8 15.0 %copy-start.21 = (s32[16]{0:T(128)S(1)}, s32[16]{0:T(128)}, u32[]{:S(2)}) copy-start(s32[16]{0:T(128)} %param.21) | copy-start | bytes 196
  97.9 23.3 %all-to-all-start.4 = ((bf16[16,32,640]{2,1,0:T(8,128)(2,1)}), bf16[16,32,640]{2,1,0:T(8,128)(2,1)}, u32[]{:S(2)}, u32[]{:S(2)}) async-start(bf16[16,32,640]{2,1,0:T(8,128)(2,1)} %add_convert_fusion), calls=%async_computation.4 | async-start | bytes 1310720 | tf_op jit(solution)/shard_map/all_to_all | solution.py:350
  111.4 0.7 copy-start.14
  111.4 1.4 copy-start.15
  111.4 1.4 copy-start.16
  112.8 9.5 %collective-permute-start.3 = (bf16[192,640]{1,0:T(8,128)(2,1)}, bf16[192,640]{1,0:T(8,128)(2,1)}, u32[]{:S(2)}, u32[]{:S(2)}) collective-permute-start(bf16[192,640]{1,0:T(8,128)(2,1)} %pad_maximum_fusion.2), channel_id=1, source_target_pairs={{0,1},{1,0},{2,3},{3,2},{4,5},{5,4},{6,7},{7,6},{8,9},{9,8},{10,11... | collective-permute-start | bytes 737288 | tf_op jit(solution)/shard_map/ppermute | solution.py:293
  121.2 2.9 %copy-start.22 = (bf16[2,1280,256]{2,1,0:T(8,128)(2,1)S(1)}, bf16[2,1280,256]{2,1,0:T(8,128)(2,1)}, u32[]{:S(2)}) copy-start(bf16[2,1280,256]{2,1,0:T(8,128)(2,1)} %param.19) | copy-start | bytes 3932164
  127.0 29.6 %all-to-all-start.2 = ((bf16[16,64,512]{2,1,0:T(8,128)(2,1)}), bf16[16,64,512]{2,1,0:T(8,128)(2,1)}, u32[]{:S(2)}, u32[]{:S(2)}) async-start(bf16[16,64,512]{2,1,0:T(8,128)(2,1)} %copy.64), calls=%async_computation.2 | async-start | bytes 2097152 | tf_op jit(solution)/shard_map/all_to_all | solution.py:403
  133.0 2.1 %copy-start.23 = (bf16[2,1280,256]{2,1,0:T(8,128)(2,1)S(1)}, bf16[2,1280,256]{2,1,0:T(8,128)(2,1)}, u32[]{:S(2)}) copy-start(bf16[2,1280,256]{2,1,0:T(8,128)(2,1)} %param.19) | copy-start | bytes 3932164
  133.1 1.6 collective-permute-start.7
  156.6 29.0 %all-to-all-start.5 = ((bf16[16,64,512]{2,1,0:T(8,128)(2,1)}), bf16[16,64,512]{2,1,0:T(8,128)(2,1)}, u32[]{:S(2)}, u32[]{:S(2)}) async-start(bf16[16,64,512]{2,1,0:T(8,128)(2,1)} %copy.69), calls=%async_computation.5 | async-start | bytes 2097152 | tf_op jit(solution)/shard_map/all_to_all | solution.py:403
  168.0 19.7 %copy-start.12 = (bf16[778,256]{1,0:T(8,128)(2,1)S(1)}, bf16[778,256]{1,0:T(8,128)(2,1)}, u32[]{:S(2)}) copy-start(bf16[778,256]{1,0:T(8,128)(2,1)} %query_ref.1) | copy-start | bytes 1195012
  193.5 1.3 copy-start.5

commit v4 on v3

--- a/solution.py
+++ b/solution.py
@@ -127,23 +127,23 @@
         MAXC * TILE, model_width
     )
     return decode(
-        [crop_norm], decoder_kv_w, vertex_queries, crop_counts, crop_owner
+        [crop_norm], lambda part: part, decoder_kv_w, vertex_queries, crop_counts, crop_owner
     ), stream_part
 
 
-def head_window(head):
-    first = head * HD // 128 * 128
-    last = -(-(head + 1) * HD // 128) * 128
-    return first, last - first, head * HD - first
-
-
-def head_attention(query, key_of, value_of, out_ref, row_slice, heads_here, keep):
-    factor = HD ** (-0.5) * LOG2E
+def head_window(head, size):
+    first = head * size // 128 * 128
+    last = -(-(head + 1) * size // 128) * 128
+    return first, last - first, head * size - first
+
+
+def head_attention(query, key_of, value_of, out_ref, row_slice, heads_here, keep, size=HD):
+    factor = size ** (-0.5) * LOG2E
     done = {}
     for head in range(heads_here):
-        first, width, start = head_window(head)
+        first, width, start = head_window(head, size)
         lane = lax.broadcasted_iota(jnp.int32, (1, width), 1)
-        inside = (lane >= start) & (lane < start + HD)
+        inside = (lane >= start) & (lane < start + size)
         q_here = query[:, first : first + width]
         q_here = jnp.where(inside, q_here, jnp.zeros_like(q_here))
         scores = lax.dot_general(
@@ -352,8 +352,8 @@
     stream_part = jnp.stack(returned, axis=1).reshape(1, patches, half)
     frame_id = lax.axis_index("frame")
     my_tiles = lax.dynamic_index_in_dim(crop_tiles, frame_id, 0, keepdims=False)
-    norms = []
-    for part in returned:
+
+    def crop_norm_of(part):
         tile_view = part.reshape(patches // TILE, TILE // CHUNKS, half)
         crop_mine = jnp.concatenate(
             [
@@ -368,11 +368,12 @@
             jnp.concatenate([crop_mine, crop_other], axis=1),
             jnp.concatenate([crop_other, crop_mine], axis=1),
         )
-        norms.append(layer_norm(crop_rows.astype(jnp.float32), decoder_gain))
-    return decode(norms, decoder_kv_w, vertex_queries, crop_counts, crop_owner), stream_part
-
-
-def decode(crop_norms, decoder_kv_w, vertex_queries, crop_counts, crop_owner):
+        return layer_norm(crop_rows.astype(jnp.float32), decoder_gain)
+
+    return decode(returned, crop_norm_of, decoder_kv_w, vertex_queries, crop_counts, crop_owner), stream_part
+
+
+def decode(parts, crop_norm_of, decoder_kv_w, vertex_queries, crop_counts, crop_owner):
     frame_id = lax.axis_index("frame")
     frames_all = crop_owner.shape[0]
     dec_local = decoder_kv_w.shape[2]
@@ -387,7 +388,12 @@
     ).astype(jnp.bfloat16)
     by_frame = choose.reshape(RCAP, frames_all, MAXC).sum(axis=2).astype(jnp.bfloat16)
     pieces = []
-    for crop_norm in crop_norms:
+    outgoing = None
+    for part in parts:
+        if outgoing is not None:
+            part, outgoing = lax.optimization_barrier((part, outgoing))
+            pieces.append(outgoing)
+        crop_norm = crop_norm_of(part)
         crop_keys = jnp.dot(crop_norm, decoder_kv_w[0], preferred_element_type=jnp.float32).astype(
             jnp.bfloat16
         )
@@ -400,11 +406,13 @@
         outgoing = jnp.einsum(
             "nm,mtc->ntc", to_owner, crop_pairs, preferred_element_type=jnp.float32
         ).astype(jnp.bfloat16)
+    pieces.append(outgoing)
+    for index, outgoing in enumerate(pieces):
         incoming = lax.all_to_all(outgoing, "frame", split_axis=0, concat_axis=0, tiled=True)
         piece = jnp.einsum(
             "rg,gtc->rtc", by_frame, incoming, preferred_element_type=jnp.float32
         ).astype(jnp.bfloat16)
-        pieces.append(piece)
+        pieces[index] = piece
     slot_pairs = jnp.concatenate(pieces, axis=1)
     if dec_local % 128 == 0:
         return vertex_decoder(slot_pairs, vertex_queries)
@@ -423,28 +431,17 @@
 
 
 def decoder_kernel(pair_ref, query_ref, out_ref):
-    width = query_ref.shape[1]
-    factor = DEC_HD ** (-0.5) * LOG2E
-    values = pair_ref[0, :, width:].T
-    lane = lax.broadcasted_iota(jnp.int32, (1, 128), 1)
-    for head in range(width // DEC_HD):
-        start = head * DEC_HD
-        first = start // 128 * 128
-        inside = (lane >= start - first) & (lane < start - first + DEC_HD)
-        keys = pair_ref[0, :, first : first + 128]
-        keys = jnp.where(inside, keys, jnp.zeros_like(keys))
-        scores = lax.dot_general(
-            keys,
-            query_ref[:, first : first + 128],
-            (((1,), (1,)), ((), ())),
-            preferred_element_type=jnp.float32,
-        )
-        top = jnp.max(scores, axis=0, keepdims=True)
-        raised = jnp.exp2((scores - top) * factor)
-        weights = (raised / jnp.sum(raised, axis=0, keepdims=True)).astype(jnp.bfloat16)
-        out_ref[0, start : start + DEC_HD, :] = jnp.dot(
-            values[start : start + DEC_HD], weights, preferred_element_type=jnp.float32
-        ).astype(jnp.bfloat16)
+    cols = query_ref.shape[1]
+    head_attention(
+        query_ref[...],
+        lambda first, width: pair_ref[0, :, first : first + width],
+        lambda first, width: pair_ref[0, :, cols + first : cols + first + width],
+        out_ref.at[0],
+        slice(None),
+        cols // DEC_HD,
+        None,
+        DEC_HD,
+    )
 
 
 def vertex_decoder(slot_pairs, queries):
@@ -457,11 +454,11 @@
             pl.BlockSpec((1, keys, both), lambda i: (i, 0, 0)),
             pl.BlockSpec((vertices, width), lambda i: (0, 0)),
         ],
-        out_specs=pl.BlockSpec((1, width, vertices), lambda i: (i, 0, 0)),
-        out_shape=jax.ShapeDtypeStruct((slots, width, vertices), jnp.bfloat16),
+        out_specs=pl.BlockSpec((1, vertices, width), lambda i: (i, 0, 0)),
+        out_shape=jax.ShapeDtypeStruct((slots, vertices, width), jnp.bfloat16),
         compiler_params=pltpu.CompilerParams(vmem_limit_bytes=32 * MIB),
         name="decoder",
-    )(slot_pairs, queries)
+    )(slot_pairs, queries).transpose(0, 2, 1)
 
 
 def solution(mesh):

time: 201 us -> 215 us (1.070)
  Pallas kernels: 50.6 us -> 59.5 us
  waiting for transfers between devices: 52.2 us -> 58 us
  local copies, waits for them, and re-layouts: 28.6 us -> 26.3 us
    pallas_call x1, Pallas kernels: 5.78 us -> 14 us  [vertex_decoder(): pl.pallas_call(decoder_kernel, grid=(slots,), in_specs=[pl.BlockSpec((1,...]
    all_to_all x2, waiting for transfers between devices: 6.96 us -> 12.1 us  [on_device_pair(): lax.all_to_all(final_mine, 'frame', split_axis=0, concat_axis=0, tiled=True)]
    optimization_barrier x0 -> x1, local copies, waits for them, and re-layouts: none -> 2.77 us  [decode(): part, outgoing = lax.optimization_barrier((part, outgoing))]
    unnamed x50 -> x46, local copies, waits for them, and re-layouts: 16.5 us -> 13.8 us
    all_to_all x2, waiting for transfers between devices: 0.01 us -> 2.45 us  [on_device_pair(): lax.all_to_all(middle.reshape(frames_all, part_rows, half), 'frame', spli...]
  transfers between devices with their start and end apart: 14 -> 14, of which waited for: 8 -> 8; matrix products, arithmetic and copies ran while one was open for 10% -> 12% of each run, Pallas kernels for 18% -> 17%
where the time goes in v4:
time: 215 us; the launch traced here: 212 us
  Pallas kernels  59.5 us (28%)
  waiting for transfers between devices  58 us (27%)
  starting transfers between devices  40.5 us (19%)
  local copies, waits for them, and re-layouts  26.3 us (12%)
  other arithmetic  14.4 us (7%)
  matrix products  7.38 us (3%)
  between operations  6.52 us (3%)
    all_to_all x2, waiting for transfers between devices, decode(): lax.all_to_all(outgoing, 'frame', split_axis=0, concat_axis=0, tiled=True)  36.3 us
    pallas_call x2, Pallas kernels, temporal_attention(): pl.pallas_call(temporal_kernel, grid=(patch_rows // PATCHES,), in_specs=[...  27.7 us
    pallas_call x2, Pallas kernels, spatial_attention(): pl.pallas_call(spatial_kernel, grid=(patches // ROWS,), in_specs=[pl.Bloc...  17.8 us
    all_to_all x2, starting transfers between devices, on_device_pair(): lax.all_to_all(middle.reshape(frames_all, part_rows, half), 'frame', spli...  14 us
    all_to_all x2, starting transfers between devices, on_device_pair(): lax.all_to_all(final_mine, 'frame', split_axis=0, concat_axis=0, tiled=True)  14 us
    pallas_call x1, Pallas kernels, vertex_decoder(): pl.pallas_call(decoder_kernel, grid=(slots,), in_specs=[pl.BlockSpec((1,...  14 us
    unnamed x46, local copies, waits for them, and re-layouts  13.8 us
    all_to_all x2, waiting for transfers between devices, on_device_pair(): lax.all_to_all(final_mine, 'frame', split_axis=0, concat_axis=0, tiled=True)  12.1 us
  transfers between devices with their start and end apart: 14, of which 8 were waited for; matrix products, arithmetic and copies ran while one was open for 12% of the time, Pallas kernels for 17%

profile of v4, /device:TPU:14, one launch (start us, length us, event | category | flops | bytes accessed | tf_op | source)
XLA Modules:
  0.0 212.5 jit_solution(8705699639078315509)
XLA Ops:
  0.6 2.6 %slice_bitcast_fusion = (bf16[1024,640]{1,0:T(8,128)(2,1)S(1)}, bf16[1,1024,1,640]{3,1,2,0:T(8,128)(2,1)S(1)}, bf16[1024,640]{1,0:T(8,128)(2,1)S(1)}) fusion(bf16[1,1024,3,640]{3,1,2,0:T(8,128)(2,1)} %param.13), kind=kLoop, calls=%fused_computation.9 | loop fusion | bytes 7864320 | tf_op jit(solution)/shard_map/squeeze | solution.py:326
  3.3 0.1 fusion.42
  3.4 0.9 copy-done.1
  4.3 0.4 copy-done.3
  4.7 0.9 copy-done.5
  5.6 8.9 %spatial.3 = (bf16[512,640]{1,0:T(8,128)(2,1)S(1)}, bf16[512,640]{1,0:T(8,128)(2,1)}) custom-call(bf16[512,640]{1,0:T(8,128)(2,1)S(1)} %bitcast.65, bf16[1024,640]{1,0:T(8,128)(2,1)S(1)} %get-tuple-element.38.k_ref, bf16[1024,640]{1,0:T(8,128)(2,1)S(1)} %get-tuple-element.36.v_ref, bf16[640,1280]{1,0:T(8,128)(2,1)S(1)} %copy-done.5), custom_call_target="tpu_custom_call" | custom-call | tf_op jit(solution)/shard_map/spatial/pallas_call | solution.py:199
  14.6 0.9 copy-done.11
  15.4 0.1 constant_dynamic-slice_fusion.2
  15.5 1.0 fusion.41
  16.5 1.4 collective-permute-done.3
  17.9 2.2 %fusion = bf16[512,640]{1,0:T(8,128)(2,1)} fusion(bf16[512,640]{1,0:T(8,128)(2,1)} %collective-permute-done.3, bf16[512,640]{1,0:T(8,128)(2,1)S(1)} %copy-done.12, bf16[16,1,32,640]{3,2,1,0:T(8,128)(2,1)S(1)} %get-tuple-element.39), kind=kLoop, calls=%fused_computation.4 | loop fusion | flops 1966080 | bytes 2621440 | tf_op jit(solution)/shard_map/convert_element_type | solution.py:298
  20.1 7.1 %all-to-all-start.2 = ((bf16[16,32,640]{2,1,0:T(8,128)(2,1)}), bf16[16,32,640]{2,1,0:T(8,128)(2,1)}, u32[]{:S(2)}, u32[]{:S(2)}) async-start(bf16[16,32,640]{2,1,0:T(8,128)(2,1)} %bitcast.71), calls=%async_computation.2 | async-start | bytes 1310720 | tf_op jit(solution)/shard_map/all_to_all | solution.py:335
  27.2 1.3 copy-done.2
  28.5 1.3 copy-done.4
  29.8 1.4 copy-done.6
  31.3 8.9 %spatial.2 = (bf16[512,640]{1,0:T(8,128)(2,1)S(1)}, bf16[512,640]{1,0:T(8,128)(2,1)}) custom-call(bf16[512,640]{1,0:T(8,128)(2,1)S(1)} %bitcast.64, bf16[1024,640]{1,0:T(8,128)(2,1)S(1)} %copy-done.4, bf16[1024,640]{1,0:T(8,128)(2,1)S(1)} %copy-done.2, bf16[640,1280]{1,0:T(8,128)(2,1)S(1)} %copy-done.6), custom_call_target="tpu_custom_call" | custom-call | tf_op jit(solution)/shard_map/spatial/pallas_call | solution.py:199
  40.1 0.8 copy-done.13
  41.0 2.5 %all-to-all-done.2.mid_mine = bf16[16,32,640]{2,1,0:T(8,128)(2,1)} async-done(((bf16[16,32,640]{2,1,0:T(8,128)(2,1)}), bf16[16,32,640]{2,1,0:T(8,128)(2,1)}, u32[]{:S(2)}, u32[]{:S(2)}) %all-to-all-start.2) | async-done | bytes 655392 | tf_op jit(solution)/shard_map/all_to_all | solution.py:335
  43.4 2.4 %fusion.1 = bf16[512,640]{1,0:T(8,128)(2,1)} fusion(bf16[512,640]{1,0:T(8,128)(2,1)S(1)} %collective-permute-done, bf16[512,640]{1,0:T(8,128)(2,1)} %copy-done.13, bf16[16,1,32,640]{3,2,1,0:T(8,128)(2,1)} %get-tuple-element.40), kind=kLoop, calls=%fused_computation.6 | loop fusion | flops 1966080 | bytes 2621440 | tf_op jit(solution)/shard_map/convert_element_type | solution.py:298
  45.8 6.9 %all-to-all-start = ((bf16[16,32,640]{2,1,0:T(8,128)(2,1)}), bf16[16,32,640]{2,1,0:T(8,128)(2,1)S(1)}, u32[]{:S(2)}, u32[]{:S(2)}) async-start(bf16[16,32,640]{2,1,0:T(8,128)(2,1)} %bitcast.70), calls=%async_computation | async-start | bytes 1310720 | tf_op jit(solution)/shard_map/all_to_all | solution.py:335
  52.7 1.4 copy-done.7
  54.2 13.6 %temporal.3 = (bf16[16,32,640]{2,1,0:T(8,128)(2,1)S(1)}, bf16[16,32,640]{2,1,0:T(8,128)(2,1)S(1)}) custom-call(bf16[16,32,640]{2,1,0:T(8,128)(2,1)} %all-to-all-done.2.mid_mine, bf16[16,32,640]{2,1,0:T(8,128)(2,1)} %collective-permute-done.4.mid_other, bf16[1,1280]{1,0:T(2,128)(2,1)S(1)} %reshape.132.gain_ref, bf16[3,1280,640]{2,1,0:T(8,128)(2,1)} %w_ref.7, ...), custom_call_target="tpu_custom_call" | custom-call | tf_op jit(solution)/shard_map/temporal/pallas_call | solution.py:271
  67.9 2.1 collective-permute-done.5
  69.9 2.2 %add_convert_fusion = bf16[16,32,640]{2,1,0:T(8,128)(2,1)} fusion(bf16[16,32,640]{2,1,0:T(8,128)(2,1)S(1)} %collective-permute-done.5, bf16[16,32,640]{2,1,0:T(8,128)(2,1)S(1)} %get-tuple-element.18, bf16[16,32,640]{2,1,0:T(8,128)(2,1)} %all-to-all-done.2.mid_mine), kind=kLoop, calls=%fused_computation.7 | loop fusion | flops 1966080 | bytes 2621440 | tf_op jit(solution)/shard_map/convert_element_type | solution.py:298
  72.2 7.1 %all-to-all-start.3 = ((bf16[16,32,640]{2,1,0:T(8,128)(2,1)}), bf16[16,32,640]{2,1,0:T(8,128)(2,1)}, u32[]{:S(2)}, u32[]{:S(2)}) async-start(bf16[16,32,640]{2,1,0:T(8,128)(2,1)} %add_convert_fusion), calls=%async_computation.3 | async-start | bytes 1310720 | tf_op jit(solution)/shard_map/all_to_all | solution.py:350
  79.3 2.1 collective-permute-done.1.mid_other
  81.3 1.4 copy-done.8
  82.8 14.1 %temporal.2 = (bf16[16,32,640]{2,1,0:T(8,128)(2,1)S(1)}, bf16[16,32,640]{2,1,0:T(8,128)(2,1)}) custom-call(bf16[16,32,640]{2,1,0:T(8,128)(2,1)S(1)} %all-to-all-done.mid_mine, bf16[16,32,640]{2,1,0:T(8,128)(2,1)S(1)} %collective-permute-done.1.mid_other, bf16[1,1280]{1,0:T(2,128)(2,1)S(1)} %reshape.132.gain_ref, bf16[3,1280,640]{2,1,0:T(8,128)(2,1)} %w_ref.7, ...), custom_call_target="tpu_custom_call" | custom-call | tf_op jit(solution)/shard_map/temporal/pallas_call | solution.py:271
  96.9 0.8 copy-done.9
  97.7 0.2 collective-permute-start.2
  97.9 0.6 fusion.43
  102.2 0.7 dynamic_slice.35
  102.9 0.2 fusion.28
  104.9 0.7 iota_compare_fusion.3
  105.7 1.1 dynamic-slice_bitcast_fusion.5
  106.7 0.7 pad_maximum_fusion.2
  107.4 0.4 collective-permute-start.6
  107.8 2.2 %add_convert_fusion.1 = bf16[16,32,640]{2,1,0:T(8,128)(2,1)} fusion(bf16[16,32,640]{2,1,0:T(8,128)(2,1)} %collective-permute-done.2, bf16[16,32,640]{2,1,0:T(8,128)(2,1)S(1)} %copy-done.10, bf16[16,32,640]{2,1,0:T(8,128)(2,1)S(1)} %all-to-all-done.mid_mine), kind=kLoop, calls=%fused_computation.8 | loop fusion | flops 1966080 | bytes 2621440 | tf_op jit(solution)/shard_map/convert_element_type | solution.py:298
  110.0 6.9 %all-to-all-start.1 = ((bf16[16,32,640]{2,1,0:T(8,128)(2,1)}), bf16[16,32,640]{2,1,0:T(8,128)(2,1)S(1)}, u32[]{:S(2)}, u32[]{:S(2)}) async-start(bf16[16,32,640]{2,1,0:T(8,128)(2,1)} %add_convert_fusion.1), calls=%async_computation.1 | async-start | bytes 1310720 | tf_op jit(solution)/shard_map/all_to_all | solution.py:350
  116.9 1.4 convert_reduce_fusion.1
  118.3 0.3 fusion.13
  118.6 0.4 convolution_convert_fusion.5
  119.0 0.4 convolution_convert_fusion.4
  119.3 1.6 convolution_convert_fusion.1
  120.9 12.1 %all-to-all-done.1 = bf16[16,32,640]{2,1,0:T(8,128)(2,1)S(1)} async-done(((bf16[16,32,640]{2,1,0:T(8,128)(2,1)}), bf16[16,32,640]{2,1,0:T(8,128)(2,1)S(1)}, u32[]{:S(2)}, u32[]{:S(2)}) %all-to-all-start.1) | async-done | bytes 655392 | tf_op jit(solution)/shard_map/all_to_all | solution.py:350
  133.1 2.8 %copy.67 = bf16[16,64,512]{2,1,0:T(8,128)(2,1)} copy(bf16[16,64,512]{2,0,1:T(8,128)(2,1)} %convolution_convert_fusion.1) | data formatting | bytes 2097152 | tf_op jit(solution)/shard_map/optimization_barrier | solution.py:394
  135.8 6.0 %all-to-all-start.4 = ((bf16[16,64,512]{2,1,0:T(8,128)(2,1)}), bf16[16,64,512]{2,1,0:T(8,128)(2,1)}, u32[]{:S(2)}, u32[]{:S(2)}) async-start(bf16[16,64,512]{2,1,0:T(8,128)(2,1)} %copy.67), calls=%async_computation.4 | async-start | bytes 2097152 | tf_op jit(solution)/shard_map/all_to_all | solution.py:411
  142.0 1.5 collective-permute-done.7
  143.5 0.2 convert_reduce_fusion
  143.7 0.3 fusion.10
  144.0 0.4 convolution_convert_fusion.3
  144.3 0.4 convolution_convert_fusion.2
  144.7 0.6 convolution_convert_fusion
  145.3 1.5 copy.71
  146.9 18.6 %all-to-all-done.4 = bf16[16,64,512]{2,1,0:T(8,128)(2,1)} async-done(((bf16[16,64,512]{2,1,0:T(8,128)(2,1)}), bf16[16,64,512]{2,1,0:T(8,128)(2,1)}, u32[]{:S(2)}, u32[]{:S(2)}) %all-to-all-start.4) | async-done | bytes 1048608 | tf_op jit(solution)/shard_map/all_to_all | solution.py:411
  165.5 5.8 %all-to-all-start.5 = ((bf16[16,64,512]{2,1,0:T(8,128)(2,1)}), bf16[16,64,512]{2,1,0:T(8,128)(2,1)}, u32[]{:S(2)}, u32[]{:S(2)}) async-start(bf16[16,64,512]{2,1,0:T(8,128)(2,1)} %copy.71), calls=%async_computation.5 | async-start | bytes 2097152 | tf_op jit(solution)/shard_map/all_to_all | solution.py:411
  171.9 0.2 select_reduce_fusion
  172.4 1.2 pad_maximum_fusion
  173.6 1.2 copy.74
  174.8 1.9 fusion.8
  176.8 17.7 %all-to-all-done.5 = bf16[16,64,512]{2,1,0:T(8,128)(2,1)} async-done(((bf16[16,64,512]{2,1,0:T(8,128)(2,1)}), bf16[16,64,512]{2,1,0:T(8,128)(2,1)}, u32[]{:S(2)}, u32[]{:S(2)}) %all-to-all-start.5) | async-done | bytes 1048608 | tf_op jit(solution)/shard_map/all_to_all | solution.py:411
  194.5 1.9 fusion.6
  196.5 14.0 %decoder.1 = bf16[4,778,256]{2,1,0:T(8,128)(2,1)S(1)} custom-call(bf16[4,128,512]{2,1,0:T(8,128)(2,1)S(1)} %pad_maximum_fusion.1.pair_ref, bf16[778,256]{1,0:T(8,128)(2,1)S(1)} %copy-done.14), custom_call_target="tpu_custom_call" | custom-call | tf_op jit(solution)/shard_map/decoder/pallas_call | solution.py:450
  210.5 2.0 copy.75
  (71 shorter events, 1.4 us)
Async XLA Ops:
  0.6 14.8 %copy-start = (bf16[1,1024,1280]{2,1,0:T(8,128)(2,1)S(1)}, bf16[1,1024,1280]{2,1,0:T(8,128)(2,1)}, u32[]{:S(2)}) copy-start(bf16[1,1024,1280]{2,1,0:T(8,128)(2,1)} %param.12) | copy-start | bytes 7864324
  3.2 1.1 copy-start.1
  3.3 1.5 copy-start.3
  3.3 2.4 %copy-start.5 = (bf16[640,1280]{1,0:T(8,128)(2,1)S(1)}, bf16[640,1280]{1,0:T(8,128)(2,1)}, u32[]{:S(2)}) copy-start(bf16[640,1280]{1,0:T(8,128)(2,1)} %w_ref.6) | copy-start | bytes 4915204
  14.5 0.9 copy-start.11
  15.4 2.4 %collective-permute-start.3 = (bf16[512,640]{1,0:T(8,128)(2,1)}, bf16[512,640]{1,0:T(8,128)(2,1)}, u32[]{:S(2)}, u32[]{:S(2)}) collective-permute-start(bf16[512,640]{1,0:T(8,128)(2,1)} %get-tuple-element.17), channel_id=1, source_target_pairs={{0,1},{1,0},{2,3},{3,2},{4,5},{5,4},{6,7},{7,6},{8,9},{9,8},{10,11... | collective-permute-start | bytes 1966088 | tf_op jit(solution)/shard_map/ppermute | solution.py:293
  15.5 2.3 %copy-start.12 = (bf16[512,640]{1,0:T(8,128)(2,1)S(1)}, bf16[512,640]{1,0:T(8,128)(2,1)}, u32[]{:S(2)}) copy-start(bf16[512,640]{1,0:T(8,128)(2,1)} %copy-done.11) | copy-start | bytes 1966084
  20.1 23.4 %all-to-all-start.2 = ((bf16[16,32,640]{2,1,0:T(8,128)(2,1)}), bf16[16,32,640]{2,1,0:T(8,128)(2,1)}, u32[]{:S(2)}, u32[]{:S(2)}) async-start(bf16[16,32,640]{2,1,0:T(8,128)(2,1)} %bitcast.71), calls=%async_computation.2 | async-start | bytes 1310720 | tf_op jit(solution)/shard_map/all_to_all | solution.py:335
  27.2 1.3 copy-start.2
  28.5 1.3 copy-start.4
  29.8 1.4 copy-start.6
  40.1 0.8 copy-start.13
  41.0 2.5 %collective-permute-start = (bf16[512,640]{1,0:T(8,128)(2,1)}, bf16[512,640]{1,0:T(8,128)(2,1)S(1)}, u32[]{:S(2)}, u32[]{:S(2)}) collective-permute-start(bf16[512,640]{1,0:T(8,128)(2,1)} %get-tuple-element.13), channel_id=1, source_target_pairs={{0,1},{1,0},{2,3},{3,2},{4,5},{5,4},{6,7},{7,6},{8,9},{9,8},{10,11... | collective-permute-start | bytes 1966088 | tf_op jit(solution)/shard_map/ppermute | solution.py:293
  43.4 9.3 %collective-permute-start.4 = (bf16[16,32,640]{2,1,0:T(8,128)(2,1)}, bf16[16,32,640]{2,1,0:T(8,128)(2,1)}, u32[]{:S(2)}, u32[]{:S(2)}) collective-permute-start(bf16[16,32,640]{2,1,0:T(8,128)(2,1)} %all-to-all-done.2.mid_mine), channel_id=1, source_target_pairs={{0,1},{1,0},{2,3},{3,2},{4,5},{5,4},{6,7},{7,6},{8,9},{9,8},{10,11... | collective-permute-start | bytes 1966088 | tf_op jit(solution)/shard_map/ppermute | solution.py:293
  45.8 6.9 %copy-start.17 = (bf16[1280]{0:T(1024)(128)(2,1)S(1)}, bf16[1280]{0:T(1024)(128)(2,1)}, u32[]{:S(2)}) copy-start(bf16[1280]{0:T(1024)(128)(2,1)} %param.15) | copy-start | bytes 7684
  45.8 26.4 %all-to-all-start = ((bf16[16,32,640]{2,1,0:T(8,128)(2,1)}), bf16[16,32,640]{2,1,0:T(8,128)(2,1)S(1)}, u32[]{:S(2)}, u32[]{:S(2)}) async-start(bf16[16,32,640]{2,1,0:T(8,128)(2,1)} %bitcast.70), calls=%async_computation | async-start | bytes 1310720 | tf_op jit(solution)/shard_map/all_to_all | solution.py:335
  52.7 1.4 copy-start.7
  67.8 2.2 %collective-permute-start.5 = (bf16[16,32,640]{2,1,0:T(8,128)(2,1)S(1)}, bf16[16,32,640]{2,1,0:T(8,128)(2,1)S(1)}, u32[]{:S(2)}, u32[]{:S(2)}) collective-permute-start(bf16[16,32,640]{2,1,0:T(8,128)(2,1)S(1)} %get-tuple-element.19), channel_id=1, source_target_pairs={{0,1},{1,0},{2,3},{3,2},{4,5},{5,4},{6,7},{7,6},{8,9},{9,8},{10,11... | collective-permute-start | bytes 1966088 | tf_op jit(solution)/shard_map/ppermute | solution.py:293
  72.2 25.7 %copy-start.18 = (s32[16,3]{0,1:T(4,128)S(1)}, s32[16,3]{0,1:T(4,128)}, u32[]{:S(2)}) copy-start(s32[16,3]{0,1:T(4,128)} %param.22) | copy-start | bytes 580
  72.2 30.1 %copy-start.16 = (bf16[1280]{0:T(1024)(128)(2,1)S(1)}, bf16[1280]{0:T(1024)(128)(2,1)}, u32[]{:S(2)}) copy-start(bf16[1280]{0:T(1024)(128)(2,1)} %param.18) | copy-start | bytes 7684
  72.2 30.1 %copy-start.19 = (s32[16]{0:T(128)S(1)}, s32[16]{0:T(128)}, u32[]{:S(2)}) copy-start(s32[16]{0:T(128)} %param.21) | copy-start | bytes 196
  72.2 30.7 %copy-start.15 = (s32[16,3]{0,1:T(4,128)S(1)}, s32[16,3]{0,1:T(4,128)}, u32[]{:S(2)}) copy-start(s32[16,3]{0,1:T(4,128)} %param.23) | copy-start | bytes 580
  72.2 33.5 %all-to-all-start.3 = ((bf16[16,32,640]{2,1,0:T(8,128)(2,1)}), bf16[16,32,640]{2,1,0:T(8,128)(2,1)}, u32[]{:S(2)}, u32[]{:S(2)}) async-start(bf16[16,32,640]{2,1,0:T(8,128)(2,1)} %add_convert_fusion), calls=%async_computation.3 | async-start | bytes 1310720 | tf_op jit(solution)/shard_map/all_to_all | solution.py:350
  79.2 2.1 collective-permute-start.1
  81.3 1.4 copy-start.8
  96.9 0.8 copy-start.9
  97.7 10.1 %collective-permute-start.2 = (bf16[16,32,640]{2,1,0:T(8,128)(2,1)}, bf16[16,32,640]{2,1,0:T(8,128)(2,1)}, u32[]{:S(2)}, u32[]{:S(2)}) collective-permute-start(bf16[16,32,640]{2,1,0:T(8,128)(2,1)} %get-tuple-element.15), channel_id=1, source_target_pairs={{0,1},{1,0},{2,3},{3,2},{4,5},{5,4},{6,7},{7,6},{8,9},{9,8},{10,11... | collective-permute-start | bytes 1966088 | tf_op jit(solution)/shard_map/ppermute | solution.py:293
  105.6 2.1 %copy-start.10 = (bf16[16,32,640]{2,1,0:T(8,128)(2,1)S(1)}, bf16[16,32,640]{2,1,0:T(8,128)(2,1)}, u32[]{:S(2)}) copy-start(bf16[16,32,640]{2,1,0:T(8,128)(2,1)} %copy-done.9) | copy-start | bytes 1966084
  107.4 9.5 %collective-permute-start.6 = (bf16[192,640]{1,0:T(8,128)(2,1)}, bf16[192,640]{1,0:T(8,128)(2,1)}, u32[]{:S(2)}, u32[]{:S(2)}) collective-permute-start(bf16[192,640]{1,0:T(8,128)(2,1)} %pad_maximum_fusion.2), channel_id=1, source_target_pairs={{0,1},{1,0},{2,3},{3,2},{4,5},{5,4},{6,7},{7,6},{8,9},{9,8},{10,11... | collective-permute-start | bytes 737288 | tf_op jit(solution)/shard_map/ppermute | solution.py:293
  110.0 23.1 %all-to-all-start.1 = ((bf16[16,32,640]{2,1,0:T(8,128)(2,1)}), bf16[16,32,640]{2,1,0:T(8,128)(2,1)S(1)}, u32[]{:S(2)}, u32[]{:S(2)}) async-start(bf16[16,32,640]{2,1,0:T(8,128)(2,1)} %add_convert_fusion.1), calls=%async_computation.1 | async-start | bytes 1310720 | tf_op jit(solution)/shard_map/all_to_all | solution.py:350
  116.9 1.7 copy-start.20
  135.8 29.6 %all-to-all-start.4 = ((bf16[16,64,512]{2,1,0:T(8,128)(2,1)}), bf16[16,64,512]{2,1,0:T(8,128)(2,1)}, u32[]{:S(2)}, u32[]{:S(2)}) async-start(bf16[16,64,512]{2,1,0:T(8,128)(2,1)} %copy.67), calls=%async_computation.4 | async-start | bytes 2097152 | tf_op jit(solution)/shard_map/all_to_all | solution.py:411
  141.9 2.1 copy-start.21
  141.9 1.6 collective-permute-start.7
  165.5 29.1 %all-to-all-start.5 = ((bf16[16,64,512]{2,1,0:T(8,128)(2,1)}), bf16[16,64,512]{2,1,0:T(8,128)(2,1)}, u32[]{:S(2)}, u32[]{:S(2)}) async-start(bf16[16,64,512]{2,1,0:T(8,128)(2,1)} %copy.71), calls=%async_computation.5 | async-start | bytes 2097152 | tf_op jit(solution)/shard_map/all_to_all | solution.py:411
  176.8 19.7 %copy-start.14 = (bf16[778,256]{1,0:T(8,128)(2,1)S(1)}, bf16[778,256]{1,0:T(8,128)(2,1)}, u32[]{:S(2)}) copy-start(bf16[778,256]{1,0:T(8,128)(2,1)} %query_ref.1) | copy-start | bytes 1195012
